TPU v7x, 32 devices: a whole 2x2x4 slice. The times are simulated.
32 devices in a mesh: tensor: 4 (over y, x), dp: 2 (over core), replica: 4 (over z).
Axes of the slice: x: 2, y: 2, z: 4, core: 2. Of those that a mesh axis runs over, the one named last changes fastest.
Arguments:
- features: bfloat16 [8, 640, 8], P(('dp', 'replica'), 'tensor'), may hold values from -6 to 6
- output_grad: bfloat16 [8, 640, 28672], P(('dp', 'replica'), None, 'tensor'), may hold values from -6 to 6
- master: float32 [8, 1, 28672], P(('dp', 'replica'), None, 'tensor'), may hold values from -1.5 to 1.5
- first_moment: float32 [8, 1, 28672], P(('dp', 'replica'), None, 'tensor'), may hold values from -0.03 to 0.03
- second_moment: float32 [8, 1, 28672], P(('dp', 'replica'), None, 'tensor'), may hold values from 1e-06 to 0.0001
- owner_map: int32 [8], replicated, may hold values from 0 to 7, each once
- step_count: int32 [1], replicated, may hold values from 1 to 99
- learning_rate: float32 [1], replicated, may hold values from 0.005 to 0.05
Outputs:
- params: bfloat16 [8, 28672], P(None, 'tensor')
- new_master: float32 [8, 1, 28672], P(('dp', 'replica'), None, 'tensor')
- new_first: float32 [8, 1, 28672], P(('dp', 'replica'), None, 'tensor')
- new_second: float32 [8, 1, 28672], P(('dp', 'replica'), None, 'tensor')
- direction: float32 [8, 1, 28672], P(('dp', 'replica'), None, 'tensor')
Inputs may be any that keep to these rules, and one draw needn't show every extreme that they name: `owner_map`: every rank owns exactly one block.
All inputs are finite; a program needn't handle non-finite values.
Results may differ from a plain program's by a relative error of at most 0.008.
Values may be sent and summed in bfloat16 or wider, within the bound.
No kernel may reach another device: no remote copies, remote signals or barrier semaphores. Data moves between devices by JAX's collectives and lax.ppermute only.
A program may use at most 64 MiB of HBM per device.

v0:
```python
import jax
import jax.numpy as jnp
from jax import lax
from jax.sharding import PartitionSpec as P

beta_first = 0.9
beta_second = 0.95
epsilon = 1e-08
decay_rate = 0.1


def adam_update(gradient, master, first_moment, second_moment, step_count, learning_rate):
    count_float = step_count[0].astype(jnp.float32)
    new_first = beta_first * first_moment + (1.0 - beta_first) * gradient
    new_second = beta_second * second_moment + (1.0 - beta_second) * gradient * gradient
    correct_first = 1.0 - jnp.power(jnp.float32(beta_first), count_float)
    correct_second = 1.0 - jnp.power(jnp.float32(beta_second), count_float)
    direction = new_first / correct_first / (jnp.sqrt(new_second / correct_second) + epsilon)
    new_master = master - learning_rate[0] * (direction + decay_rate * master)
    return (new_master, new_first, new_second, direction)


def on_device(
    features, output_grad, master, first_moment, second_moment, owner_map, step_count, learning_rate
):
    gathered = lax.all_gather(features, "tensor", axis=1, tiled=True)
    activations = gathered[0]
    grads_out = output_grad[0]
    owners = owner_map.shape[0]
    own_rows = master.shape[1]
    columns = master.shape[2]
    dp_count = lax.axis_size("dp")
    replica_count = lax.axis_size("replica")
    tok_total = activations.shape[0] * dp_count * replica_count
    inverse = jnp.zeros((owners,), jnp.int32).at[owner_map].set(jnp.arange(owners, dtype=jnp.int32))
    column_order = (
        inverse[:, None] * own_rows + jnp.arange(own_rows, dtype=jnp.int32)[None, :]
    ).reshape(-1)
    ordered = jnp.take(activations, column_order, axis=1)
    partial_value = lax.dot_general(
        ordered, grads_out, (((0,), (0,)), ((), ())), preferred_element_type=jnp.float32
    )
    rounded = lax.optimization_barrier(partial_value.astype(jnp.bfloat16))
    summed = lax.psum_scatter(
        rounded.astype(jnp.float32), ("dp", "replica"), scatter_dimension=0, tiled=True
    )
    gradient = summed[None] / tok_total
    new_master, new_first, new_second, direction = adam_update(
        gradient, master, first_moment, second_moment, step_count, learning_rate
    )
    everyone = lax.all_gather(
        new_master.astype(jnp.bfloat16), ("dp", "replica"), axis=0, tiled=True
    )
    params = jnp.take(everyone, owner_map, axis=0).reshape(owners * own_rows, columns)
    return (params, new_master, new_first, new_second, direction)


def solution(mesh):
    in_specs = (
        P(("dp", "replica"), "tensor", None),
        P(("dp", "replica"), None, "tensor"),
        P(("dp", "replica"), None, "tensor"),
        P(("dp", "replica"), None, "tensor"),
        P(("dp", "replica"), None, "tensor"),
        P(),
        P(),
        P(),
    )
    out_specs = (
        P(None, "tensor"),
        P(("dp", "replica"), None, "tensor"),
        P(("dp", "replica"), None, "tensor"),
        P(("dp", "replica"), None, "tensor"),
        P(("dp", "replica"), None, "tensor"),
    )
    return jax.shard_map(
        on_device, mesh=mesh, in_specs=in_specs, out_specs=out_specs, check_vma=False
    )
```

profile of v0, /device:TPU:0, one launch (start us, length us, event | category | flops | bytes accessed | tf_op | source)
XLA Modules:
  0.0 80.0 jit_solution(12893353032148865616)
XLA Ops:
  0.6 0.0 copy-start.4
  0.6 0.0 copy-start
  0.7 0.0 copy-start.2
  0.7 0.0 copy-start.1
  0.7 0.7 compare_select_fusion.1
  1.4 0.6 scatter_custom_fusion
  2.0 0.8 %copy.26 = bf16[1,160,8]{2,0,1:T(2,128)(2,1)S(1)} copy(bf16[1,160,8]{1,2,0:T(8,128)(2,1)} %param.8) | data formatting | bytes 5120 | tf_op args[0]
  2.8 10.7 %all_gather.6 = bf16[1,640,8]{2,0,1:T(2,128)(2,1)S(1)} all-gather(bf16[1,160,8]{2,0,1:T(2,128)(2,1)S(1)} %copy.26), channel_id=1, replica_groups=mesh['tensor'=4,'dp'=2,'replica'=4] {'tensor'}, dimensions={1}, use_global_device_ids=true | all-gather | bytes 12800 | tf_op jit(solution)/shard_map/all_gather | solution.py:26
  13.5 0.1 copy.27
  13.6 0.0 copy-start.3
  13.6 0.6 gather_fusion
  14.2 4.9 %fusion.2 = bf16[8,7168]{1,0:T(8,128)(2,1)S(1)} fusion(bf16[1,640,7168]{2,1,0:T(8,128)(2,1)} %param.9, bf16[8,640]{1,0:T(8,128)(2,1)S(1)} %gather_fusion, pred[8]{0:T(512)(128)(4,1)S(1)} %compare_and_fusion), kind=kOutput, calls=%fused_computation.5 | convolution fusion | flops 73462784 | bytes 9299976 | tf_op jit(solution)/shard_map/dot_general | solution.py:40
  19.2 31.5 %all-reduce.2 = f32[8,7168]{1,0:T(8,128)S(1)} all-reduce(bf16[8,7168]{1,0:T(8,128)(2,1)S(1)} %fusion.2), channel_id=2, replica_groups=mesh['tensor'=4,'dp'=2,'replica'=4] {'dp','replica'}, use_global_device_ids=true, to_apply=%region_1.2.clone | all-reduce | flops 57344 | bytes 344064
  51.4 0.0 copy-done.4
  51.4 0.6 dynamic-slice
  52.7 0.0 copy-done
  52.7 0.0 copy-done.2
  52.7 0.0 copy-done.1
  52.7 1.5 %fusion.11 = (bf16[1,1,7168]{2,1,0:T(2,128)(2,1)S(1)}, f32[1,1,7168]{2,1,0:T(1,128)}, f32[1,1,7168]{2,1,0:T(1,128)}, f32[1,1,7168]{2,1,0:T(1,128)}, f32[1,1,7168]{2,1,0:T(1,128)}) fusion(f32[1,1,7168]{2,1,0:T(1,128)S(1)} %copy-done, f32[]{:T(128)} %bitcast.19, f32[]{:T(128)} %bitcast.6, f32[]{:T(128)} %bitcast.4, f32[8,7168]{1,0:T(8,128)S(1)} %all-reduce.2, ...), kind=kLoop, calls=%fused_computation.24 | loop fusion | flops 121856 | bytes 243728 | tf_op jit(solution)/shard_map/convert_element_type | solution.py:52
  54.2 24.4 %all_gather.7 = bf16[8,1,7168]{2,1,0:T(2,128)(2,1)S(1)} all-gather(bf16[1,1,7168]{2,1,0:T(2,128)(2,1)S(1)} %get-tuple-element.10), channel_id=1, replica_groups=mesh['tensor'=4,'dp'=2,'replica'=4] {'dp','replica'}, dimensions={0}, use_global_device_ids=true | all-gather | bytes 129024 | tf_op jit(solution)/shard_map/all_gather | solution.py:51
  78.6 0.6 gather_fusion.1
  79.2 0.0 copy-done.3
  79.2 0.7 broadcast_select_fusion
  (7 shorter events, 0.1 us)
Async XLA Ops:
  0.6 50.8 %copy-start.4 = (u32[32]{0:T(128)S(1)}, u32[32]{0:T(128)}, u32[]{:S(2)}) copy-start(u32[32]{0:T(128)} %constant.63) | copy-start | bytes 388
  0.6 52.0 %copy-start = (f32[1,1,7168]{2,1,0:T(1,128)S(1)}, f32[1,1,7168]{2,1,0:T(1,128)}, u32[]{:S(2)}) copy-start(f32[1,1,7168]{2,1,0:T(1,128)} %param.10) | copy-start | bytes 86020
  0.7 52.0 %copy-start.2 = (f32[1,1,7168]{2,1,0:T(1,128)S(1)}, f32[1,1,7168]{2,1,0:T(1,128)}, u32[]{:S(2)}) copy-start(f32[1,1,7168]{2,1,0:T(1,128)} %param.11) | copy-start | bytes 86020
  0.7 52.0 %copy-start.1 = (f32[1,1,7168]{2,1,0:T(1,128)S(1)}, f32[1,1,7168]{2,1,0:T(1,128)}, u32[]{:S(2)}) copy-start(f32[1,1,7168]{2,1,0:T(1,128)} %param.12) | copy-start | bytes 86020
  13.6 65.6 %copy-start.3 = (s32[8]{0:T(128)S(1)}, s32[8]{0:T(128)}, u32[]{:S(2)}) copy-start(s32[8]{0:T(128)} %param.13) | copy-start | bytes 100
where the time goes:
time: 81.4 us; the launch traced here: 80 us
  blocking collectives  66.5 us (82%)
  matrix products  4.94 us (6%)
  local copies, waits for them, and re-layouts  3.42 us (4%)
  other arithmetic  2.89 us (4%)
  between operations  2.16 us (3%)
    unnamed x1, blocking collectives  31.5 us
    all_gather x1, blocking collectives, on_device(): lax.all_gather(new_master.astype(jnp.bfloat16), ('dp', 'replica'), axis=0...  24.4 us
    all_gather x1, blocking collectives, on_device(): gathered = lax.all_gather(features, 'tensor', axis=1, tiled=True)  10.7 us
    dot_general x1, matrix products, on_device(): lax.dot_general(ordered, grads_out, (((0,), (0,)), ((), ())), preferred_e...  4.94 us

commit v1 on v0

v1 whole, which is shorter than its diff:
```python
import functools
import math
import jax
import jax.numpy as jnp
from jax import lax
from jax.experimental import pallas as pl
from jax.experimental.pallas import tpu as pltpu
from jax.sharding import PartitionSpec as P

beta_first = 0.9
beta_second = 0.95
epsilon = 1e-08
decay_rate = 0.1
RANK_AXES = ("dp", "replica")
SHARED = 2


def chip_masks(chips):
    rest = [m for m in range(1, chips) if m != SHARED]
    return [(rest[i], rest[i + 1]) for i in range(0, len(rest), 2)]


def where_am_i():
    replicas = lax.axis_size("replica")
    dp = lax.axis_index("dp")
    core = lax.rem(dp, 2)
    chip = lax.div(dp, 2) * replicas + lax.axis_index("replica")
    return core, chip


def rank_of(chip, core):
    replicas = lax.axis_size("replica")
    return (lax.div(chip, replicas) * 2 + core) * replicas + lax.rem(chip, replicas)


def swap_cores(x):
    count = lax.axis_size("dp")
    return lax.ppermute(x, "dp", [(i, i ^ 1) for i in range(count)])


def swap_chips(x, mask_even, mask_odd):
    replicas = lax.axis_size("replica")
    pairs = []
    for dp in range(lax.axis_size("dp")):
        for z in range(replicas):
            chip = (dp // 2 * replicas + z) ^ (mask_odd if dp % 2 else mask_even)
            pairs.append((dp * replicas + z, (chip // replicas * 2 + dp % 2) * replicas + chip % replicas))
    return lax.ppermute(x, RANK_AXES, pairs)


def swap_tensor(x, mask):
    return lax.ppermute(x, "tensor", [(i, i ^ mask) for i in range(lax.axis_size("tensor"))])


def owners_of(row, chips, core, chip):
    half = chips - 2
    pairs = chip_masks(chips)
    mask = jnp.where(row < 2 * half + 2, SHARED, 0)
    for p, (even, odd) in enumerate(pairs):
        mine = jnp.where(core == 0, even, odd)
        theirs = jnp.where(core == 0, odd, even)
        mask = jnp.where(lax.div(row, 2) == p, mine, mask)
        mask = jnp.where(lax.div(row, 2) == p + len(pairs), theirs, mask)
    return rank_of(jnp.bitwise_xor(chip, mask), lax.rem(row, 2))


def matmul_kernel(chips, chunk, owner_ref, *refs):
    shards = len(refs) - 5
    f_refs, (g_ref, keep_ref, send_ref, keep_half_ref, send_half_ref) = refs[:shards], refs[shards:]
    rows = f_refs[0].shape[0]
    half = g_ref.shape[1] // 2
    served = keep_ref.shape[0]
    core, chip = where_am_i()
    place = lax.axis_index("tensor")
    blocks = [f_ref[...].astype(jnp.float32) for f_ref in f_refs]
    ordered = []
    for b in range(shards):
        block = blocks[b]
        for t in range(1, shards):
            block = jnp.where(place == t, blocks[b ^ t], block)
        ordered.append(block)
    features = jnp.concatenate(ordered, axis=1).astype(jnp.bfloat16)
    row = lax.broadcasted_iota(jnp.int32, (rows, rows), 0)
    pick = owners_of(row, chips, core, chip) == owner_ref[...]
    features = jnp.dot(
        pick.astype(jnp.float32).astype(jnp.bfloat16), features, preferred_element_type=jnp.float32
    ).astype(jnp.bfloat16)
    for side, half_ref in enumerate((keep_half_ref, send_half_ref)):
        base = (core if side == 0 else 1 - core) * half
        for k in range(half // chunk):
            columns = pl.ds(pl.multiple_of(base + k * chunk, chunk), chunk)
            part = jnp.dot(features, g_ref[:, columns], preferred_element_type=jnp.float32)
            part = part.astype(jnp.bfloat16).astype(jnp.float32)
            keep_ref[:, columns] = part[:served]
            send_ref[:, columns] = part[served : 2 * served].astype(jnp.bfloat16)
            half_ref[:, pl.ds(k * chunk, chunk)] = part[2 * served :].astype(half_ref.dtype)


def load_kernel(source_ref, out_ref, sem):
    copy = pltpu.make_async_copy(source_ref, out_ref, sem)
    copy.start()
    copy.wait()


def gradient_rows(core, chunk, k, side, sums_ref, other_ref, half_ref, other_half_ref, tokens):
    half = half_ref.shape[1]
    base = (core if side == 0 else 1 - core) * half
    columns = pl.ds(pl.multiple_of(base + k * chunk, chunk), chunk)
    place = pl.ds(k * chunk, chunk)
    total = sums_ref[:, columns] + other_ref[:, columns]
    total = total + (half_ref, other_half_ref)[side][:, place]
    return columns, place, total / tokens


def corrections(step_ref):
    count = jnp.full((1, 128), step_ref[0], jnp.int32).astype(jnp.float32)
    first = 1.0 - jnp.exp(count * math.log(beta_first))
    second = 1.0 - jnp.exp(count * math.log(beta_second))
    return first[:, :1], second[:, :1]


def adam(gradient, master, first_moment, second_moment, correct_first, correct_second, rate):
    new_first = beta_first * first_moment + (1.0 - beta_first) * gradient
    new_second = beta_second * second_moment + (1.0 - beta_second) * gradient * gradient
    direction = new_first / correct_first / (jnp.sqrt(new_second / correct_second) + epsilon)
    new_master = master - rate * (direction + decay_rate * master)
    return new_master, new_first, new_second, direction


def params_kernel(chunk, tokens, step_ref, rate_ref, sums_ref, sums_other_ref, half_ref, other_half_ref, *refs):
    state_refs, (params_ref, params_half_ref) = refs[:6], refs[6:]
    core, _ = where_am_i()
    corrected = corrections(step_ref)
    for side in range(2):
        for k in range(half_ref.shape[1] // chunk):
            columns, place, gradient = gradient_rows(
                core, chunk, k, side, sums_ref, sums_other_ref, half_ref, other_half_ref, tokens
            )
            state = []
            for own_ref, other_ref in zip(state_refs[:3], state_refs[3:]):
                own, other = own_ref[:, columns], other_ref[:, columns]
                low, high = jnp.where(core == 0, own, other), jnp.where(core == 0, other, own)
                state.append(jnp.concatenate([low, high], axis=0))
            value = adam(gradient, *state, *corrected, rate_ref[0])[0].astype(jnp.bfloat16)
            params_ref[:, columns] = value
            if side == 0:
                params_half_ref[:, place] = value


def state_kernel(chunk, tokens, step_ref, rate_ref, sums_ref, other_ref, half_ref, other_half_ref, *refs):
    state_refs, out_refs = refs[:3], refs[3:]
    core, _ = where_am_i()
    corrected = corrections(step_ref)
    for side in range(2):
        for k in range(half_ref.shape[1] // chunk):
            columns, _, gradient = gradient_rows(
                core, chunk, k, side, sums_ref, other_ref, half_ref, other_half_ref, tokens
            )
            gradient = jnp.where(core == 0, gradient[:1], gradient[1:])
            values = adam(gradient, *[ref[:, columns] for ref in state_refs], *corrected, rate_ref[0])
            for ref, value in zip(out_refs, values):
                ref[:, columns] = value


def order_kernel(chips, chunk, owner_ref, own_ref, near_ref, far_ref, half_ref, other_half_ref, out_ref):
    core, chip = where_am_i()
    rows = out_ref.shape[0]
    half = half_ref.shape[1]
    served = near_ref.shape[0]
    column = lax.broadcasted_iota(jnp.int32, (rows, rows), 1)
    owner = jnp.broadcast_to(owner_ref[...], (rows, rows)).T
    ranks = owners_of(column, chips, core, chip)
    flipped = owners_of(column, chips, 1 - core, chip)

    def pick(table, first, count):
        return (table == owner).astype(jnp.float32).astype(jnp.bfloat16)[:, first : first + count]

    near = pick(ranks, 0, served)
    far = pick(flipped, 0, served)
    shared = pick(ranks, 2 * served, 2)
    own = pick(ranks, 2 * served + 2, 2)
    for side in range(2):
        base = (core if side == 0 else 1 - core) * half
        for k in range(half // chunk):
            columns = pl.ds(pl.multiple_of(base + k * chunk, chunk), chunk)
            place = pl.ds(k * chunk, chunk)
            total = jnp.dot(own, own_ref[:, columns], preferred_element_type=jnp.float32)
            total += jnp.dot(near, near_ref[:, columns], preferred_element_type=jnp.float32)
            total += jnp.dot(far, far_ref[:, columns], preferred_element_type=jnp.float32)
            total += jnp.dot(
                shared, (half_ref, other_half_ref)[side][:, place], preferred_element_type=jnp.float32
            )
            out_ref[:, columns] = total.astype(jnp.bfloat16)


VMEM = pl.BlockSpec(memory_space=pltpu.VMEM)
SMEM = pl.BlockSpec(memory_space=pltpu.SMEM)


def call(kernel, outs, specs, name, limit=4 << 20):
    return pl.pallas_call(
        kernel,
        out_shape=[jax.ShapeDtypeStruct(shape, dtype) for shape, dtype in outs],
        in_specs=specs,
        out_specs=[VMEM] * len(outs),
        compiler_params=pltpu.CompilerParams(vmem_limit_bytes=limit),
        name=name,
    )


def on_device(
    features, output_grad, master, first_moment, second_moment, owner_map, step_count, learning_rate
):
    replicas = lax.axis_size("replica")
    chips = lax.axis_size("dp") // 2 * replicas
    shards = lax.axis_size("tensor")
    _, tokens, columns = output_grad.shape
    rows = features.shape[2]
    ranks = owner_map.shape[0]
    half = columns // 2
    served = chips - 2
    chunk = 512 if half % 512 == 0 else 128
    pairs = chip_masks(chips)
    f32, bf16 = jnp.float32, jnp.bfloat16

    mine = features[0].T
    blocks = [mine] + [swap_tensor(mine, t) for t in range(1, shards)]
    state = [x.reshape(1, columns) for x in (master, first_moment, second_moment)]
    partner = [swap_cores(x) for x in state]
    owners = owner_map.reshape(1, ranks)

    loaded = pl.pallas_call(
        load_kernel,
        out_shape=jax.ShapeDtypeStruct((tokens, columns), bf16),
        in_specs=[pl.BlockSpec(memory_space=pl.ANY)],
        out_specs=VMEM,
        scratch_shapes=[pltpu.SemaphoreType.DMA],
        compiler_params=pltpu.CompilerParams(vmem_limit_bytes=4 << 20),
        cost_estimate=pl.CostEstimate(
            flops=0, bytes_accessed=4 * tokens * columns, transcendentals=0
        ),
        name="load_output_grad",
    )(output_grad[0])
    keep, send, keep_half, send_half = call(
        functools.partial(matmul_kernel, chips, chunk),
        [((served, columns), f32), ((served, columns), bf16), ((4, half), f32), ((4, half), bf16)],
        [VMEM] * (shards + 2),
        "partial_gradient",
    )(owners, *blocks, loaded)
    sums = (keep + swap_cores(send).astype(f32)).astype(bf16)
    sums_half = keep_half + swap_cores(send_half).astype(f32)
    arrived = [swap_chips(sums[2 * p : 2 * p + 2], *pair) for p, pair in enumerate(pairs)]
    arrived_half = swap_chips(sums_half[:2].astype(bf16), SHARED, SHARED)
    row_sums = sum(x.astype(f32) for x in arrived)
    row_half = arrived_half.astype(f32) + sums_half[2:]
    grads = (row_sums, swap_cores(row_sums), row_half, swap_cores(row_half))

    total = float(tokens * ranks)
    params, params_half = call(
        functools.partial(params_kernel, chunk, total),
        [((2, columns), bf16), ((2, half), bf16)],
        [SMEM, SMEM] + [VMEM] * 10,
        "chip_params",
    )(step_count, learning_rate, *grads, *state, *partner)
    outs = call(
        functools.partial(state_kernel, chunk, total),
        [((1, columns), f32)] * 4,
        [SMEM, SMEM] + [VMEM] * 7,
        "own_state",
    )(step_count, learning_rate, *grads, *state)
    near = jnp.concatenate([swap_chips(params, *pair) for pair in pairs], axis=0)
    near_half = swap_chips(params_half, SHARED, SHARED)
    ordered = call(
        functools.partial(order_kernel, chips, chunk),
        [((rows, columns), bf16)],
        [VMEM] * 6,
        "row_order",
    )(owners, params, near, swap_cores(near), near_half, swap_cores(near_half))
    return (ordered[0], *[x.reshape(master.shape) for x in outs])


def solution(mesh):
    in_specs = (
        P(("dp", "replica"), "tensor", None),
        P(("dp", "replica"), None, "tensor"),
        P(("dp", "replica"), None, "tensor"),
        P(("dp", "replica"), None, "tensor"),
        P(("dp", "replica"), None, "tensor"),
        P(),
        P(),
        P(),
    )
    out_specs = (
        P(None, "tensor"),
        P(("dp", "replica"), None, "tensor"),
        P(("dp", "replica"), None, "tensor"),
        P(("dp", "replica"), None, "tensor"),
        P(("dp", "replica"), None, "tensor"),
    )
    return jax.shard_map(
        on_device, mesh=mesh, in_specs=in_specs, out_specs=out_specs, check_vma=False
    )
```

time: 81.4 us -> 29.3 us (0.36); the launches traced: 80 us -> 29.1 us
  blocking collectives: 66.5 us -> 0 us
  starting transfers between devices: 0 us -> 14.8 us
  matrix products: 4.94 us -> 0 us
  Pallas kernels: 0 us -> 4.32 us
  waiting for transfers between devices: 0 us -> 4.16 us
  other arithmetic: 2.89 us -> 0.1 us
    all_gather x2 -> x0, blocking collectives: 35.1 us -> none  [the longest x1 24.4 us: on_device(): lax.all_gather(new_master.astype(jnp.bfloat16), ('dp', 'replica'), axis=0...]
    unnamed x1 -> x0, blocking collectives: 31.5 us -> none
    ppermute x0 -> x16, starting transfers between devices: none -> 14.8 us  [the longest x4 6.73 us: swap_chips(): return lax.ppermute(x, RANK_AXES, pairs)]
    dot_general x1 -> x0, matrix products: 4.94 us -> none  [on_device(): lax.dot_general(ordered, grads_out, (((0,), (0,)), ((), ())), preferred_e...]
    pallas_call x0 -> x5, Pallas kernels: none -> 4.32 us  [the longest x1 1.47 us: on_device(): call(functools.partial(matmul_kernel, chips, chunk), [((served, columns),...]
    ppermute x0 -> x16, waiting for transfers between devices: none -> 4.16 us  [the longest x4 2.91 us: swap_chips(): return lax.ppermute(x, RANK_AXES, pairs)]
    unnamed x13 -> x12, local copies, waits for them, and re-layouts: 1.49 us -> 3.63 us
    select_n x3 -> x0, other arithmetic: 1.41 us -> none  [the longest x2 1.41 us: on_device(): jnp.take(everyone, owner_map, axis=0).reshape(owners * own_rows, columns)]
  transfers between devices with their start and end apart: 0 -> 16, of which waited for: 0 -> 6; matrix products, arithmetic and copies ran while one was open for 0% -> 0% of each run, Pallas kernels for 0% -> 5%
where the time goes in v1:
time: 29.3 us; the launch traced here: 29.1 us
  starting transfers between devices  14.8 us (51%)
  Pallas kernels  4.32 us (15%)
  waiting for transfers between devices  4.16 us (14%)
  local copies, waits for them, and re-layouts  3.64 us (12%)
  between operations  2.08 us (7%)
    ppermute x4, starting transfers between devices, swap_chips(): return lax.ppermute(x, RANK_AXES, pairs)  6.73 us
    ppermute x3, starting transfers between devices, swap_tensor(): lax.ppermute(x, 'tensor', [(i, i ^ mask) for i in range(lax.axis_size('te...  4.54 us
    unnamed x12, local copies, waits for them, and re-layouts  3.63 us
    ppermute x9, starting transfers between devices, swap_cores(): return lax.ppermute(x, 'dp', [(i, i ^ 1) for i in range(count)])  3.55 us
    ppermute x4, waiting for transfers between devices, swap_chips(): return lax.ppermute(x, RANK_AXES, pairs)  2.91 us
    pallas_call x1, Pallas kernels, on_device(): call(functools.partial(matmul_kernel, chips, chunk), [((served, columns),...  1.47 us
    pallas_call x1, Pallas kernels, on_device(): call(functools.partial(order_kernel, chips, chunk), [((rows, columns), bf...  1.24 us
    ppermute x9, waiting for transfers between devices, swap_cores(): return lax.ppermute(x, 'dp', [(i, i ^ 1) for i in range(count)])  0.84 us
  transfers between devices with their start and end apart: 16, of which 6 were waited for; matrix products, arithmetic and copies ran while one was open for 0% of the time, Pallas kernels for 5%

profile of v1, /device:TPU:0, one launch (start us, length us, event | category | flops | bytes accessed | tf_op | source)
XLA Modules:
  0.0 29.1 jit_solution(10947934781095480892)
XLA Ops:
  0.6 3.0 %collective-permute-start = (bf16[8,160]{1,0:T(8,128)(2,1)}, bf16[8,160]{1,0:T(8,128)(2,1)S(1)}, u32[]{:S(2)}, u32[]{:S(2)}) collective-permute-start(bf16[8,160]{1,0:T(8,128)(2,1)} %bitcast.22), channel_id=1, source_target_pairs={{0,8},{8,0},{16,24},{24,16},{1,9},{9,1},{17,25},{25,17},{2,10},{10... | collective-permute-start | bytes 7688 | tf_op jit(solution)/shard_map/ppermute | solution.py:52
  3.6 1.5 %collective-permute-start.1 = (bf16[8,160]{1,0:T(8,128)(2,1)}, bf16[8,160]{1,0:T(8,128)(2,1)S(1)}, u32[]{:S(2)}, u32[]{:S(2)}) collective-permute-start(bf16[8,160]{1,0:T(8,128)(2,1)} %bitcast.23), channel_id=1, source_target_pairs={{0,16},{8,24},{16,0},{24,8},{1,17},{9,25},{17,1},{25,9},{2,18},{10... | collective-permute-start | bytes 7688 | tf_op jit(solution)/shard_map/ppermute | solution.py:52
  5.2 0.0 collective-permute-start.2
  5.2 3.6 %copy-done = bf16[1,640,7168]{2,1,0:T(8,128)(2,1)S(1)} copy-done((bf16[1,640,7168]{2,1,0:T(8,128)(2,1)S(1)}, bf16[1,640,7168]{2,1,0:T(8,128)(2,1)}, u32[]{:S(2)}) %copy-start) | copy-done | bytes 9175064
  8.8 0.6 %load_output_grad.1.refs_4_ = bf16[640,7168]{1,0:T(8,128)(2,1)S(1)} custom-call(bf16[640,7168]{1,0:T(8,128)(2,1)S(1)} %bitcast.12), custom_call_target="tpu_custom_call" | custom-call | bytes 18350080 | tf_op jit(solution)/shard_map/load_output_grad/pallas_call | solution.py:232
  9.4 0.0 copy-start.2
  9.4 0.0 copy-start.3
  9.4 0.0 copy-start.1
  9.4 0.0 collective-permute-done.refs_1_
  9.5 0.0 collective-permute-done.1.refs_2_
  9.5 0.4 %collective-permute-done.2.refs_3_ = bf16[8,160]{1,0:T(8,128)(2,1)S(1)} collective-permute-done((bf16[8,160]{1,0:T(8,128)(2,1)}, bf16[8,160]{1,0:T(8,128)(2,1)S(1)}, u32[]{:S(2)}, u32[]{:S(2)}) %collective-permute-start.2) | collective-permute-done | bytes 2592 | tf_op jit(solution)/shard_map/ppermute | solution.py:52
  9.9 1.5 %partial_gradient.1 = (f32[2,7168]{1,0:T(2,128)S(1)}, bf16[2,7168]{1,0:T(2,128)(2,1)S(1)}, f32[4,3584]{1,0:T(4,128)S(1)}, bf16[4,3584]{1,0:T(4,128)(2,1)S(1)}) custom-call(s32[1,8]{1,0:T(1,128)S(1)} %bitcast.26, bf16[8,160]{1,0:T(8,128)(2,1)S(1)} %bitcast.25, bf16[8,160]{1,0:T(8,128)(2,1)S(1)} %collective-permute-done.refs_1_, ...), custom_call_target="tpu_custom_call" | custom-call | tf_op jit(solution)/shard_map/partial_gradient/pallas_call | solution.py:244
  11.3 0.0 collective-permute-start.3
  11.4 0.5 %collective-permute-start.6 = (bf16[4,3584]{1,0:T(4,128)(2,1)S(1)}, bf16[4,3584]{1,0:T(4,128)(2,1)S(1)}, u32[]{:S(2)}, u32[]{:S(2)}) collective-permute-start(bf16[4,3584]{1,0:T(4,128)(2,1)S(1)} %get-tuple-element.18), channel_id=1, source_target_pairs={{0,4},{4,0},{1,5},{5,1},{2,6},{6,2},{3,7},{7,3},{8,12},{12,8},{9,1... | collective-permute-start | bytes 86024 | tf_op jit(solution)/shard_map/ppermute | solution.py:38
  11.9 0.7 %collective-permute-done.3 = bf16[2,7168]{1,0:T(2,128)(2,1)S(1)} collective-permute-done((bf16[2,7168]{1,0:T(2,128)(2,1)S(1)}, bf16[2,7168]{1,0:T(2,128)(2,1)S(1)}, u32[]{:S(2)}, u32[]{:S(2)}) %collective-permute-start.3) | collective-permute-done | bytes 28704 | tf_op jit(solution)/shard_map/ppermute | solution.py:38
  12.6 1.7 %collective-permute-start.4 = (bf16[2,7168]{1,0:T(2,128)(2,1)S(1)}, bf16[2,7168]{1,0:T(2,128)(2,1)S(1)}, u32[]{:S(2)}, u32[]{:S(2)}) collective-permute-start(bf16[2,7168]{1,0:T(2,128)(2,1)S(1)} %add_convert_fusion), channel_id=1, source_target_pairs={{0,1},{1,0},{2,3},{3,2},{4,7},{5,6},{6,5},{7,4},{8,9},{9,8},{10,11... | collective-permute-start | bytes 86024 | tf_op jit(solution)/shard_map/ppermute | solution.py:48
  14.4 2.7 %collective-permute-start.7 = (bf16[2,3584]{1,0:T(2,128)(2,1)S(1)}, bf16[2,3584]{1,0:T(2,128)(2,1)S(1)}, u32[]{:S(2)}, u32[]{:S(2)}) collective-permute-start(bf16[2,3584]{1,0:T(2,128)(2,1)S(1)} %slice.13), channel_id=1, source_target_pairs={{0,2},{1,3},{2,0},{3,1},{4,6},{5,7},{6,4},{7,5},{8,10},{9,11},{10,... | collective-permute-start | bytes 43016 | tf_op jit(solution)/shard_map/ppermute | solution.py:48
  17.0 0.5 %collective-permute-start.11 = (f32[1,7168]{1,0:T(1,128)S(1)}, f32[1,7168]{1,0:T(1,128)S(1)}, u32[]{:S(2)}, u32[]{:S(2)}) collective-permute-start(f32[1,7168]{1,0:T(1,128)S(1)} %bitcast.19), channel_id=1, source_target_pairs={{0,4},{4,0},{1,5},{5,1},{2,6},{6,2},{3,7},{7,3},{8,12},{12,8},{9,1... | collective-permute-start | bytes 86024 | tf_op jit(solution)/shard_map/ppermute | solution.py:38
  17.5 0.1 collective-permute-start.9
  17.6 0.5 %collective-permute-start.5 = (f32[2,7168]{1,0:T(2,128)S(1)}, f32[2,7168]{1,0:T(2,128)S(1)}, u32[]{:S(2)}, u32[]{:S(2)}) collective-permute-start(f32[2,7168]{1,0:T(2,128)S(1)} %convert_element_type.18.sums_ref), channel_id=1, source_target_pairs={{0,4},{4,0},{1,5},{5,1},{2,6},{6,2},{3,7},{7,3},{8,12},{12,8},{9,1... | collective-permute-start | bytes 172040 | tf_op jit(solution)/shard_map/ppermute | solution.py:38
  18.1 1.0 %collective-permute-done.7 = bf16[2,3584]{1,0:T(2,128)(2,1)S(1)} collective-permute-done((bf16[2,3584]{1,0:T(2,128)(2,1)S(1)}, bf16[2,3584]{1,0:T(2,128)(2,1)S(1)}, u32[]{:S(2)}, u32[]{:S(2)}) %collective-permute-start.7) | collective-permute-done | bytes 14368 | tf_op jit(solution)/shard_map/ppermute | solution.py:48
  19.2 0.7 %collective-permute-start.8 = (f32[2,3584]{1,0:T(2,128)S(1)}, f32[2,3584]{1,0:T(2,128)S(1)}, u32[]{:S(2)}, u32[]{:S(2)}) collective-permute-start(f32[2,3584]{1,0:T(2,128)S(1)} %slice_add_fusion.half_ref), channel_id=1, source_target_pairs={{0,4},{4,0},{1,5},{5,1},{2,6},{6,2},{3,7},{7,3},{8,12},{12,8},{9,1... | collective-permute-start | bytes 86024 | tf_op jit(solution)/shard_map/ppermute | solution.py:38
  21.2 0.3 %chip_params.1 = (bf16[2,7168]{1,0:T(2,128)(2,1)S(1)}, bf16[2,3584]{1,0:T(2,128)(2,1)S(1)}) custom-call(s32[1]{0:T(128)S(6)} %copy.13.step_ref, f32[1]{0:T(128)S(6)} %copy.14.rate_ref, f32[2,7168]{1,0:T(2,128)S(1)} %convert_element_type.18.sums_ref, f32[2,7168]{1,0:T(2,128)S(1)} %collective-permute-done.5.sums_other_ref.other_ref, ...), custom_call_target="tpu_custom_call" | custom-call | tf_op jit(solution)/shard_map/chip_params/pallas_call | solution.py:259
  21.5 0.1 collective-permute-start.12
  21.6 2.3 %collective-permute-start.14 = (bf16[2,3584]{1,0:T(2,128)(2,1)S(1)}, bf16[2,3584]{1,0:T(2,128)(2,1)S(1)}, u32[]{:S(2)}, u32[]{:S(2)}) collective-permute-start(bf16[2,3584]{1,0:T(2,128)(2,1)S(1)} %get-tuple-element.20), channel_id=1, source_target_pairs={{0,2},{1,3},{2,0},{3,1},{4,6},{5,7},{6,4},{7,5},{8,10},{9,11},{10,... | collective-permute-start | bytes 43016 | tf_op jit(solution)/shard_map/ppermute | solution.py:48
  23.9 1.6 %collective-permute-done.12.near_ref = bf16[2,7168]{1,0:T(2,128)(2,1)S(1)} collective-permute-done((bf16[2,7168]{1,0:T(2,128)(2,1)S(1)}, bf16[2,7168]{1,0:T(2,128)(2,1)S(1)}, u32[]{:S(2)}, u32[]{:S(2)}) %collective-permute-start.12) | collective-permute-done | bytes 28704 | tf_op jit(solution)/shard_map/ppermute | solution.py:48
  25.5 0.7 %collective-permute-start.13 = (bf16[2,7168]{1,0:T(2,128)(2,1)S(1)}, bf16[2,7168]{1,0:T(2,128)(2,1)S(1)}, u32[]{:S(2)}, u32[]{:S(2)}) collective-permute-start(bf16[2,7168]{1,0:T(2,128)(2,1)S(1)} %collective-permute-done.12.near_ref), channel_id=1, source_target_pairs={{0,4},{4,0},{1,5},{5,1},{2,6},{6,2},{3,7},{7,3},{8,12},{12,8},{9,1... | collective-permute-start | bytes 86024 | tf_op jit(solution)/shard_map/ppermute | solution.py:38
  26.2 0.3 %collective-permute-done.14.half_ref = bf16[2,3584]{1,0:T(2,128)(2,1)S(1)} collective-permute-done((bf16[2,3584]{1,0:T(2,128)(2,1)S(1)}, bf16[2,3584]{1,0:T(2,128)(2,1)S(1)}, u32[]{:S(2)}, u32[]{:S(2)}) %collective-permute-start.14) | collective-permute-done | bytes 14368 | tf_op jit(solution)/shard_map/ppermute | solution.py:48
  26.5 0.6 %collective-permute-start.15 = (bf16[2,3584]{1,0:T(2,128)(2,1)S(1)}, bf16[2,3584]{1,0:T(2,128)(2,1)S(1)}, u32[]{:S(2)}, u32[]{:S(2)}) collective-permute-start(bf16[2,3584]{1,0:T(2,128)(2,1)S(1)} %collective-permute-done.14.half_ref), channel_id=1, source_target_pairs={{0,4},{4,0},{1,5},{5,1},{2,6},{6,2},{3,7},{7,3},{8,12},{12,8},{9,1... | collective-permute-start | bytes 43016 | tf_op jit(solution)/shard_map/ppermute | solution.py:38
  27.0 0.7 %own_state.1 = (f32[1,7168]{1,0:T(1,128)}, f32[1,7168]{1,0:T(1,128)}, f32[1,7168]{1,0:T(1,128)}, f32[1,7168]{1,0:T(1,128)}) custom-call(s32[1]{0:T(128)S(6)} %copy.13.step_ref, f32[1]{0:T(128)S(6)} %copy.14.rate_ref, f32[2,7168]{1,0:T(2,128)S(1)} %convert_element_type.18.sums_ref, f32[2,7168]{1,0:T(2,128)S(1)} %collective-permute-done.5.sums_other_ref.other_ref, ...), custom_call_target="tpu_custom_call" | custom-call | tf_op jit(solution)/shard_map/own_state/pallas_call | solution.py:265
  27.7 0.1 collective-permute-done.15.other_half_ref
  27.9 1.2 %row_order.1 = bf16[8,7168]{1,0:T(8,128)(2,1)} custom-call(s32[1,8]{1,0:T(1,128)S(1)} %bitcast.27, bf16[2,7168]{1,0:T(2,128)(2,1)S(1)} %get-tuple-element.19.own_ref, bf16[2,7168]{1,0:T(2,128)(2,1)S(1)} %collective-permute-done.12.near_ref, bf16[2,7168]{1,0:T(2,128)(2,1)S(1)} %collective-permute-done.13.far_ref, ...), custom_call_target="tpu_custom_call" | custom-call | tf_op jit(solution)/shard_map/row_order/pallas_call | solution.py:273
  (22 shorter events, 0.1 us)
Async XLA Ops:
  0.6 8.8 %collective-permute-start = (bf16[8,160]{1,0:T(8,128)(2,1)}, bf16[8,160]{1,0:T(8,128)(2,1)S(1)}, u32[]{:S(2)}, u32[]{:S(2)}) collective-permute-start(bf16[8,160]{1,0:T(8,128)(2,1)} %bitcast.22), channel_id=1, source_target_pairs={{0,8},{8,0},{16,24},{24,16},{1,9},{9,1},{17,25},{25,17},{2,10},{10... | collective-permute-start | bytes 7688 | tf_op jit(solution)/shard_map/ppermute | solution.py:52
  3.6 5.8 %collective-permute-start.1 = (bf16[8,160]{1,0:T(8,128)(2,1)}, bf16[8,160]{1,0:T(8,128)(2,1)S(1)}, u32[]{:S(2)}, u32[]{:S(2)}) collective-permute-start(bf16[8,160]{1,0:T(8,128)(2,1)} %bitcast.23), channel_id=1, source_target_pairs={{0,16},{8,24},{16,0},{24,8},{1,17},{9,25},{17,1},{25,9},{2,18},{10... | collective-permute-start | bytes 7688 | tf_op jit(solution)/shard_map/ppermute | solution.py:52
  5.2 4.7 %collective-permute-start.2 = (bf16[8,160]{1,0:T(8,128)(2,1)}, bf16[8,160]{1,0:T(8,128)(2,1)S(1)}, u32[]{:S(2)}, u32[]{:S(2)}) collective-permute-start(bf16[8,160]{1,0:T(8,128)(2,1)} %bitcast.24), channel_id=1, source_target_pairs={{0,24},{8,16},{16,8},{24,0},{1,25},{9,17},{17,9},{25,1},{2,26},{10... | collective-permute-start | bytes 7688 | tf_op jit(solution)/shard_map/ppermute | solution.py:52
  5.2 3.6 %copy-start = (bf16[1,640,7168]{2,1,0:T(8,128)(2,1)S(1)}, bf16[1,640,7168]{2,1,0:T(8,128)(2,1)}, u32[]{:S(2)}) copy-start(bf16[1,640,7168]{2,1,0:T(8,128)(2,1)} %param.9) | copy-start | bytes 27525124
  8.8 1.1 %copy-start.4 = (bf16[1,160,8]{1,2,0:T(8,128)(2,1)S(1)}, bf16[1,160,8]{1,2,0:T(8,128)(2,1)}, u32[]{:S(2)}) copy-start(bf16[1,160,8]{1,2,0:T(8,128)(2,1)} %param.8) | copy-start | bytes 7684
  8.8 1.1 %copy-start.5 = (s32[8]{0:T(128)S(1)}, s32[8]{0:T(128)}, u32[]{:S(2)}) copy-start(s32[8]{0:T(128)} %param.13) | copy-start | bytes 100
  9.4 7.6 %copy-start.2 = (f32[1,1,7168]{2,1,0:T(1,128)S(1)}, f32[1,1,7168]{2,1,0:T(1,128)}, u32[]{:S(2)}) copy-start(f32[1,1,7168]{2,1,0:T(1,128)} %param.11) | copy-start | bytes 86020
  9.4 7.6 %copy-start.3 = (f32[1,1,7168]{2,1,0:T(1,128)S(1)}, f32[1,1,7168]{2,1,0:T(1,128)}, u32[]{:S(2)}) copy-start(f32[1,1,7168]{2,1,0:T(1,128)} %param.12) | copy-start | bytes 86020
  9.4 8.1 %copy-start.1 = (f32[1,1,7168]{2,1,0:T(1,128)S(1)}, f32[1,1,7168]{2,1,0:T(1,128)}, u32[]{:S(2)}) copy-start(f32[1,1,7168]{2,1,0:T(1,128)} %param.10) | copy-start | bytes 86020
  11.3 1.2 %collective-permute-start.3 = (bf16[2,7168]{1,0:T(2,128)(2,1)S(1)}, bf16[2,7168]{1,0:T(2,128)(2,1)S(1)}, u32[]{:S(2)}, u32[]{:S(2)}) collective-permute-start(bf16[2,7168]{1,0:T(2,128)(2,1)S(1)} %get-tuple-element.16), channel_id=1, source_target_pairs={{0,4},{4,0},{1,5},{5,1},{2,6},{6,2},{3,7},{7,3},{8,12},{12,8},{9,1... | collective-permute-start | bytes 86024 | tf_op jit(solution)/shard_map/ppermute | solution.py:38
  11.4 3.0 %collective-permute-start.6 = (bf16[4,3584]{1,0:T(4,128)(2,1)S(1)}, bf16[4,3584]{1,0:T(4,128)(2,1)S(1)}, u32[]{:S(2)}, u32[]{:S(2)}) collective-permute-start(bf16[4,3584]{1,0:T(4,128)(2,1)S(1)} %get-tuple-element.18), channel_id=1, source_target_pairs={{0,4},{4,0},{1,5},{5,1},{2,6},{6,2},{3,7},{7,3},{8,12},{12,8},{9,1... | collective-permute-start | bytes 86024 | tf_op jit(solution)/shard_map/ppermute | solution.py:38
  12.6 5.0 %collective-permute-start.4 = (bf16[2,7168]{1,0:T(2,128)(2,1)S(1)}, bf16[2,7168]{1,0:T(2,128)(2,1)S(1)}, u32[]{:S(2)}, u32[]{:S(2)}) collective-permute-start(bf16[2,7168]{1,0:T(2,128)(2,1)S(1)} %add_convert_fusion), channel_id=1, source_target_pairs={{0,1},{1,0},{2,3},{3,2},{4,7},{5,6},{6,5},{7,4},{8,9},{9,8},{10,11... | collective-permute-start | bytes 86024 | tf_op jit(solution)/shard_map/ppermute | solution.py:48
  14.4 4.8 %collective-permute-start.7 = (bf16[2,3584]{1,0:T(2,128)(2,1)S(1)}, bf16[2,3584]{1,0:T(2,128)(2,1)S(1)}, u32[]{:S(2)}, u32[]{:S(2)}) collective-permute-start(bf16[2,3584]{1,0:T(2,128)(2,1)S(1)} %slice.13), channel_id=1, source_target_pairs={{0,2},{1,3},{2,0},{3,1},{4,6},{5,7},{6,4},{7,5},{8,10},{9,11},{10,... | collective-permute-start | bytes 43016 | tf_op jit(solution)/shard_map/ppermute | solution.py:48
  17.0 4.2 %collective-permute-start.10 = (f32[1,7168]{1,0:T(1,128)S(1)}, f32[1,7168]{1,0:T(1,128)S(1)}, u32[]{:S(2)}, u32[]{:S(2)}) collective-permute-start(f32[1,7168]{1,0:T(1,128)S(1)} %bitcast.16), channel_id=1, source_target_pairs={{0,4},{4,0},{1,5},{5,1},{2,6},{6,2},{3,7},{7,3},{8,12},{12,8},{9,1... | collective-permute-start | bytes 86024 | tf_op jit(solution)/shard_map/ppermute | solution.py:38
  17.0 4.2 %collective-permute-start.11 = (f32[1,7168]{1,0:T(1,128)S(1)}, f32[1,7168]{1,0:T(1,128)S(1)}, u32[]{:S(2)}, u32[]{:S(2)}) collective-permute-start(f32[1,7168]{1,0:T(1,128)S(1)} %bitcast.19), channel_id=1, source_target_pairs={{0,4},{4,0},{1,5},{5,1},{2,6},{6,2},{3,7},{7,3},{8,12},{12,8},{9,1... | collective-permute-start | bytes 86024 | tf_op jit(solution)/shard_map/ppermute | solution.py:38
  17.5 3.7 %collective-permute-start.9 = (f32[1,7168]{1,0:T(1,128)S(1)}, f32[1,7168]{1,0:T(1,128)S(1)}, u32[]{:S(2)}, u32[]{:S(2)}) collective-permute-start(f32[1,7168]{1,0:T(1,128)S(1)} %bitcast.13), channel_id=1, source_target_pairs={{0,4},{4,0},{1,5},{5,1},{2,6},{6,2},{3,7},{7,3},{8,12},{12,8},{9,1... | collective-permute-start | bytes 86024 | tf_op jit(solution)/shard_map/ppermute | solution.py:38
  17.6 3.6 %collective-permute-start.5 = (f32[2,7168]{1,0:T(2,128)S(1)}, f32[2,7168]{1,0:T(2,128)S(1)}, u32[]{:S(2)}, u32[]{:S(2)}) collective-permute-start(f32[2,7168]{1,0:T(2,128)S(1)} %convert_element_type.18.sums_ref), channel_id=1, source_target_pairs={{0,4},{4,0},{1,5},{5,1},{2,6},{6,2},{3,7},{7,3},{8,12},{12,8},{9,1... | collective-permute-start | bytes 172040 | tf_op jit(solution)/shard_map/ppermute | solution.py:38
  19.2 2.1 %collective-permute-start.8 = (f32[2,3584]{1,0:T(2,128)S(1)}, f32[2,3584]{1,0:T(2,128)S(1)}, u32[]{:S(2)}, u32[]{:S(2)}) collective-permute-start(f32[2,3584]{1,0:T(2,128)S(1)} %slice_add_fusion.half_ref), channel_id=1, source_target_pairs={{0,4},{4,0},{1,5},{5,1},{2,6},{6,2},{3,7},{7,3},{8,12},{12,8},{9,1... | collective-permute-start | bytes 86024 | tf_op jit(solution)/shard_map/ppermute | solution.py:38
  21.5 3.9 %collective-permute-start.12 = (bf16[2,7168]{1,0:T(2,128)(2,1)S(1)}, bf16[2,7168]{1,0:T(2,128)(2,1)S(1)}, u32[]{:S(2)}, u32[]{:S(2)}) collective-permute-start(bf16[2,7168]{1,0:T(2,128)(2,1)S(1)} %get-tuple-element.19.own_ref), channel_id=1, source_target_pairs={{0,1},{1,0},{2,3},{3,2},{4,7},{5,6},{6,5},{7,4},{8,9},{9,8},{10,11... | collective-permute-start | bytes 86024 | tf_op jit(solution)/shard_map/ppermute | solution.py:48
  21.6 4.8 %collective-permute-start.14 = (bf16[2,3584]{1,0:T(2,128)(2,1)S(1)}, bf16[2,3584]{1,0:T(2,128)(2,1)S(1)}, u32[]{:S(2)}, u32[]{:S(2)}) collective-permute-start(bf16[2,3584]{1,0:T(2,128)(2,1)S(1)} %get-tuple-element.20), channel_id=1, source_target_pairs={{0,2},{1,3},{2,0},{3,1},{4,6},{5,7},{6,4},{7,5},{8,10},{9,11},{10,... | collective-permute-start | bytes 43016 | tf_op jit(solution)/shard_map/ppermute | solution.py:48
  25.5 2.4 %collective-permute-start.13 = (bf16[2,7168]{1,0:T(2,128)(2,1)S(1)}, bf16[2,7168]{1,0:T(2,128)(2,1)S(1)}, u32[]{:S(2)}, u32[]{:S(2)}) collective-permute-start(bf16[2,7168]{1,0:T(2,128)(2,1)S(1)} %collective-permute-done.12.near_ref), channel_id=1, source_target_pairs={{0,4},{4,0},{1,5},{5,1},{2,6},{6,2},{3,7},{7,3},{8,12},{12,8},{9,1... | collective-permute-start | bytes 86024 | tf_op jit(solution)/shard_map/ppermute | solution.py:38
  26.5 1.4 %collective-permute-start.15 = (bf16[2,3584]{1,0:T(2,128)(2,1)S(1)}, bf16[2,3584]{1,0:T(2,128)(2,1)S(1)}, u32[]{:S(2)}, u32[]{:S(2)}) collective-permute-start(bf16[2,3584]{1,0:T(2,128)(2,1)S(1)} %collective-permute-done.14.half_ref), channel_id=1, source_target_pairs={{0,4},{4,0},{1,5},{5,1},{2,6},{6,2},{3,7},{7,3},{8,12},{12,8},{9,1... | collective-permute-start | bytes 43016 | tf_op jit(solution)/shard_map/ppermute | solution.py:38

commit v2 on v0

v2 whole, which is shorter than its diff:
```python
import functools
import math
import jax
import jax.numpy as jnp
from jax import lax
from jax.experimental import pallas as pl
from jax.experimental.pallas import tpu as pltpu
from jax.sharding import PartitionSpec as P

beta_first = 0.9
beta_second = 0.95
epsilon = 1e-08
decay_rate = 0.1
f32, bf16 = jnp.float32, jnp.bfloat16
RANK_AXES = ("dp", "replica")
SHARED = 1


def chip_masks(chips):
    rest = [m for m in range(1, chips) if m != SHARED]
    return [(rest[i], rest[i + 1]) for i in range(0, len(rest), 2)]


def where_am_i():
    replicas = lax.axis_size("replica")
    dp = lax.axis_index("dp")
    core = lax.rem(dp, 2)
    chip = lax.div(dp, 2) * replicas + lax.axis_index("replica")
    return core, chip


def rank_of(chip, core):
    replicas = lax.axis_size("replica")
    return (lax.div(chip, replicas) * 2 + core) * replicas + lax.rem(chip, replicas)


def swap_cores(x):
    count = lax.axis_size("dp")
    return lax.ppermute(x, "dp", [(i, i ^ 1) for i in range(count)])


def swap_chips(x, mask_even, mask_odd):
    replicas = lax.axis_size("replica")
    pairs = []
    for dp in range(lax.axis_size("dp")):
        for z in range(replicas):
            chip = (dp // 2 * replicas + z) ^ (mask_odd if dp % 2 else mask_even)
            pairs.append((dp * replicas + z, (chip // replicas * 2 + dp % 2) * replicas + chip % replicas))
    return lax.ppermute(x, RANK_AXES, pairs)


def swap_tensor(x, mask):
    return lax.ppermute(x, "tensor", [(i, i ^ mask) for i in range(lax.axis_size("tensor"))])


def owners_of(row, chips, core, chip):
    half = chips - 2
    pairs = chip_masks(chips)
    mask = jnp.where(row < 2 * half + 2, SHARED, 0)
    for p, (even, odd) in enumerate(pairs):
        mine = jnp.where(core == 0, even, odd)
        theirs = jnp.where(core == 0, odd, even)
        mask = jnp.where(lax.div(row, 2) == p, mine, mask)
        mask = jnp.where(lax.div(row, 2) == p + len(pairs), theirs, mask)
    return rank_of(jnp.bitwise_xor(chip, mask), lax.rem(row, 2))


def halves(core, half, chunk, k):
    mine = pl.ds(pl.multiple_of(core * half + k * chunk, chunk), chunk)
    other = pl.ds(pl.multiple_of((1 - core) * half + k * chunk, chunk), chunk)
    return mine, other, pl.ds(k * chunk, chunk)


def owners_kernel(chips, out_ref):
    core, chip = where_am_i()
    out_ref[...] = owners_of(lax.broadcasted_iota(jnp.int32, out_ref.shape, 0), chips, core, chip)


def ordered(table_ref, owner_ref, features):
    pick = (table_ref[...] == owner_ref[...]).astype(f32).astype(bf16)
    return jnp.dot(pick, features.astype(bf16), preferred_element_type=f32).astype(bf16)


def token_rows(depth, mask, count=1):
    first = jnp.bitwise_xor(lax.axis_index("tensor"), mask)
    if count > 1:
        first = first - lax.rem(first, count)
    return pl.ds(pl.multiple_of(first * depth, 32), count * depth)


def own_kernel(chunk, table_ref, owner_ref, feature_ref, g_ref, *refs):
    (total_ref,) = refs
    features = ordered(table_ref, owner_ref, feature_ref[...])
    held = token_rows(feature_ref.shape[1], 0)
    for k in range(total_ref.shape[1] // chunk):
        columns = pl.ds(k * chunk, chunk)
        total_ref[:, columns] = jnp.dot(features, g_ref[held, columns], preferred_element_type=f32)


def pair_kernel(chunk, table_ref, owner_ref, even_ref, odd_ref, g_ref, before_ref, total_ref):
    low = lax.rem(lax.axis_index("tensor"), 2)
    even, odd = even_ref[...].astype(f32), odd_ref[...].astype(f32)
    blocks = [jnp.where(low == 0, even, odd), jnp.where(low == 0, odd, even)]
    features = ordered(table_ref, owner_ref, jnp.concatenate(blocks, axis=1))
    held = token_rows(even_ref.shape[1], 2, 2)
    for k in range(total_ref.shape[1] // chunk):
        columns = pl.ds(k * chunk, chunk)
        part = jnp.dot(features, g_ref[held, columns], preferred_element_type=f32)
        total_ref[:, columns] = before_ref[:, columns] + part


def last_kernel(chips, chunk, table_ref, owner_ref, feature_ref, g_ref, before_ref, *refs):
    own_refs, partner_refs, (keep_ref, send_ref, *state_refs) = refs[:3], refs[3:6], refs[6:]
    features = ordered(table_ref, owner_ref, feature_ref[...])
    held = token_rows(feature_ref.shape[1], 1)
    half = keep_ref.shape[1]
    served = chips - 2
    core, _ = where_am_i()
    for k in range(half // chunk):
        *sides, place = halves(core, half, chunk, k)
        mine, other = [
            (jnp.dot(features, g_ref[held, columns], preferred_element_type=f32) + before_ref[:, columns])
            .astype(bf16)
            .astype(f32)
            for columns in sides
        ]
        keep, send = [], []
        for p in range(0, served, 2):
            keep += [other[p : p + 2], mine[p : p + 2]]
            send += [mine[served + p : served + p + 2], other[served + p : served + p + 2]]
        keep_ref[:, place] = jnp.concatenate(keep + [mine[2 * served :]], axis=0)
        send_ref[:, place] = jnp.concatenate(send + [other[2 * served :]], axis=0).astype(bf16)
    for own_ref, partner_ref, ref in zip(own_refs, partner_refs, state_refs):
        own, partner = own_ref[...], partner_ref[...]
        ref[:1] = jnp.where(core == 0, own, partner)
        ref[1:] = jnp.where(core == 0, partner, own)


def corrections(step_ref):
    count = jnp.full((1, 128), step_ref[0], jnp.int32).astype(f32)
    first = 1.0 - jnp.exp(count * math.log(beta_first))
    second = 1.0 - jnp.exp(count * math.log(beta_second))
    return first[:, :1], second[:, :1]


def adam(gradient, master, first_moment, second_moment, correct_first, correct_second, rate):
    new_first = beta_first * first_moment + (1.0 - beta_first) * gradient
    new_second = beta_second * second_moment + (1.0 - beta_second) * gradient * gradient
    direction = new_first / correct_first / (jnp.sqrt(new_second / correct_second) + epsilon)
    new_master = master - rate * (direction + decay_rate * master)
    return new_master, new_first, new_second, direction


def chip_gradients(sums, others, tokens):
    return (sums[2:] + others[:2]) / tokens, (sums[:2] + others[2:]) / tokens


def params_kernel(chunk, tokens, step_ref, rate_ref, sums_ref, others_ref, *refs):
    state_refs, (params_ref, params_half_ref) = refs[:3], refs[3:]
    core, _ = where_am_i()
    corrected = corrections(step_ref)
    half = sums_ref.shape[1]
    for k in range(half // chunk):
        *sides, place = halves(core, half, chunk, k)
        values = []
        for columns, gradient in zip(sides, chip_gradients(sums_ref[:, place], others_ref[:, place], tokens)):
            state = [ref[:, columns] for ref in state_refs]
            values.append(adam(gradient, *state, *corrected, rate_ref[0])[0])
        params_ref[:, place] = jnp.concatenate(values[::-1], axis=0).astype(bf16)
        params_half_ref[:, place] = values[0].astype(bf16)


def state_kernel(chunk, tokens, step_ref, rate_ref, sums_ref, others_ref, *refs):
    state_refs, out_refs = refs[:3], refs[3:]
    core, _ = where_am_i()
    corrected = corrections(step_ref)
    half = sums_ref.shape[1]
    for k in range(half // chunk):
        *sides, place = halves(core, half, chunk, k)
        for columns, gradient in zip(sides, chip_gradients(sums_ref[:, place], others_ref[:, place], tokens)):
            gradient = jnp.where(core == 0, gradient[:1], gradient[1:])
            values = adam(gradient, *[ref[:, columns] for ref in state_refs], *corrected, rate_ref[0])
            for ref, value in zip(out_refs, values):
                ref[:, columns] = value


def picker(chips, rows, owner_ref, core, chip):
    column = lax.broadcasted_iota(jnp.int32, (rows, rows), 0)
    hot = (owners_of(column, chips, core, chip) == owner_ref[...]).astype(f32).T
    return hot.astype(bf16)


def early_kernel(chips, chunk, owner_ref, own_ref, half_ref, *refs):
    near_refs, total_ref = refs[:-1], refs[-1]
    core, chip = where_am_i()
    half = half_ref.shape[1]
    served = chips - 2
    pick = picker(chips, total_ref.shape[0], owner_ref, core, chip)
    own = pick[:, 2 * served + 2 :]
    shared = pick[:, 2 * served : 2 * served + 2]
    for k in range(half // chunk):
        mine, other, place = halves(core, half, chunk, k)
        rows = own_ref[:, place].astype(f32)
        total = jnp.dot(shared, half_ref[:, place], preferred_element_type=f32)
        total += jnp.dot(own, rows[2:].astype(bf16), preferred_element_type=f32)
        total_other = jnp.dot(own, rows[:2].astype(bf16), preferred_element_type=f32)
        for p, near_ref in enumerate(near_refs):
            near = pick[:, 2 * p : 2 * p + 2]
            rows = near_ref[:, place].astype(f32)
            total += jnp.dot(near, rows[2:].astype(bf16), preferred_element_type=f32)
            total_other += jnp.dot(near, rows[:2].astype(bf16), preferred_element_type=f32)
        total_ref[:, mine] = total
        total_ref[:, other] = total_other


def order_kernel(chips, chunk, owner_ref, total_ref, half_ref, *refs):
    far_refs, out_ref = refs[:-1], refs[-1]
    core, chip = where_am_i()
    half = half_ref.shape[1]
    served = chips - 2
    pick = picker(chips, total_ref.shape[0], owner_ref, core, chip)
    shared = pick[:, 2 * served : 2 * served + 2]
    for k in range(half // chunk):
        mine, other, place = halves(core, half, chunk, k)
        total = total_ref[:, mine]
        total_other = total_ref[:, other] + jnp.dot(shared, half_ref[:, place], preferred_element_type=f32)
        for p, far_ref in enumerate(far_refs):
            far = pick[:, served + 2 * p : served + 2 * p + 2]
            rows = far_ref[:, place].astype(f32)
            total += jnp.dot(far, rows[:2].astype(bf16), preferred_element_type=f32)
            total_other += jnp.dot(far, rows[2:].astype(bf16), preferred_element_type=f32)
        out_ref[:, mine] = total.astype(bf16)
        out_ref[:, other] = total_other.astype(bf16)


VMEM = pl.BlockSpec(memory_space=pltpu.VMEM)
SMEM = pl.BlockSpec(memory_space=pltpu.SMEM)


def call(kernel, outs, specs, name, cost=None):
    return pl.pallas_call(
        kernel,
        out_shape=[jax.ShapeDtypeStruct(shape, dtype) for shape, dtype in outs],
        in_specs=specs,
        out_specs=[VMEM] * len(outs),
        compiler_params=pltpu.CompilerParams(vmem_limit_bytes=4 << 20),
        cost_estimate=cost,
        name=name,
    )


def on_device(
    features, output_grad, master, first_moment, second_moment, owner_map, step_count, learning_rate
):
    replicas = lax.axis_size("replica")
    chips = lax.axis_size("dp") // 2 * replicas
    _, tokens, columns = output_grad.shape
    rows = features.shape[2]
    ranks = owner_map.shape[0]
    half = columns // 2
    served = chips - 2
    chunk = 512 if half % 512 == 0 else 128
    pairs = chip_masks(chips)
    source = output_grad[0]
    owners = owner_map.reshape(1, ranks)

    mine = features[0].T
    diagonal, next_two, next_one = [swap_tensor(mine, mask) for mask in (3, 2, 1)]
    state = [x.reshape(1, columns) for x in (master, first_moment, second_moment)]
    (table,) = call(
        functools.partial(owners_kernel, chips),
        [((rows, rows), jnp.int32)],
        [],
        "owners",
        pl.CostEstimate(flops=3_500_000_000, bytes_accessed=0, transcendentals=0),
    )()
    total = ((rows, columns), f32)
    (part,) = call(functools.partial(own_kernel, chunk), [total], [VMEM] * 4, "own_tokens")(
        table, owners, mine, source
    )
    partner = [swap_cores(x) for x in state]
    (part,) = call(functools.partial(pair_kernel, chunk), [total], [VMEM] * 6, "pair_tokens")(
        table, owners, next_two, diagonal, source, part
    )
    keep, send, *state_rows = call(
        functools.partial(last_kernel, chips, chunk),
        [((2 * served + 4, half), f32), ((2 * served + 4, half), bf16)] + [((2, columns), f32)] * 3,
        [VMEM] * 11,
        "last_tokens",
    )(table, owners, next_one, source, part, *state, *partner)

    sums = keep + swap_cores(send).astype(f32)
    arrived = [swap_chips(sums[4 * p : 4 * p + 4].astype(bf16), *pair) for p, pair in enumerate(pairs)]
    arrived_half = swap_chips(sums[2 * served : 2 * served + 2].astype(bf16), SHARED, SHARED)
    sums_half = arrived_half.astype(f32) + sums[2 * served + 2 :]
    arrived = sum(x.astype(f32) for x in arrived)
    chip_sums = jnp.concatenate([arrived[:2], arrived[2:] + sums_half], axis=0)
    grads = (chip_sums, swap_cores(chip_sums))

    count = float(tokens * ranks)
    params, params_half = call(
        functools.partial(params_kernel, chunk, count),
        [((4, half), bf16), ((2, half), bf16)],
        [SMEM, SMEM] + [VMEM] * 5,
        "chip_params",
    )(step_count, learning_rate, *grads, *state_rows)
    outs = call(
        functools.partial(state_kernel, chunk, count),
        [((1, columns), f32)] * 4,
        [SMEM, SMEM] + [VMEM] * 5,
        "own_state",
    )(step_count, learning_rate, *grads, *state)
    near = [swap_chips(params, *pair) for pair in pairs]
    near_half = swap_chips(params_half, SHARED, SHARED)
    far = [swap_cores(x) for x in near]
    far_half = swap_cores(near_half)
    (early,) = call(
        functools.partial(early_kernel, chips, chunk), [total], [VMEM] * (3 + len(near)), "early_rows"
    )(owners, params, near_half, *near)
    (params,) = call(
        functools.partial(order_kernel, chips, chunk),
        [((rows, columns), bf16)],
        [VMEM] * (3 + len(far)),
        "row_order",
    )(owners, early, far_half, *far)
    return (params, *[x.reshape(master.shape) for x in outs])


def solution(mesh):
    in_specs = (
        P(("dp", "replica"), "tensor", None),
        P(("dp", "replica"), None, "tensor"),
        P(("dp", "replica"), None, "tensor"),
        P(("dp", "replica"), None, "tensor"),
        P(("dp", "replica"), None, "tensor"),
        P(),
        P(),
        P(),
    )
    out_specs = (
        P(None, "tensor"),
        P(("dp", "replica"), None, "tensor"),
        P(("dp", "replica"), None, "tensor"),
        P(("dp", "replica"), None, "tensor"),
        P(("dp", "replica"), None, "tensor"),
    )
    return jax.shard_map(
        on_device, mesh=mesh, in_specs=in_specs, out_specs=out_specs, check_vma=False
    )
```

time: 81.4 us -> 27.2 us (0.33); the launches traced: 80 us -> 27 us
  blocking collectives: 66.5 us -> 0 us
  starting transfers between devices: 0 us -> 13 us
  waiting for transfers between devices: 0 us -> 7.51 us
  matrix products: 4.94 us -> 0 us
  Pallas kernels: 0 us -> 4.26 us
  local copies, waits for them, and re-layouts: 3.42 us -> 0.07 us
  other arithmetic: 2.89 us -> 0.09 us
    all_gather x2 -> x0, blocking collectives: 35.1 us -> none  [the longest x1 24.4 us: on_device(): lax.all_gather(new_master.astype(jnp.bfloat16), ('dp', 'replica'), axis=0...]
    unnamed x1 -> x0, blocking collectives: 31.5 us -> none
    ppermute x0 -> x14, starting transfers between devices: none -> 13 us  [the longest x4 7.35 us: swap_chips(): return lax.ppermute(x, RANK_AXES, pairs)]
    ppermute x0 -> x14, waiting for transfers between devices: none -> 7.51 us  [the longest x4 4.18 us: swap_chips(): return lax.ppermute(x, RANK_AXES, pairs)]
    dot_general x1 -> x0, matrix products: 4.94 us -> none  [on_device(): lax.dot_general(ordered, grads_out, (((0,), (0,)), ((), ())), preferred_e...]
    pallas_call x0 -> x8, Pallas kernels: none -> 4.26 us  [the longest x1 1.03 us: on_device(): call(functools.partial(order_kernel, chips, chunk), [((rows, columns), bf...]
    unnamed x13 -> x12, local copies, waits for them, and re-layouts: 1.49 us -> 0.03 us
    convert_element_type x1, other arithmetic: 1.45 us -> 0.01 us  [on_device(): arrived = sum((x.astype(f32) for x in arrived))]
  transfers between devices with their start and end apart: 0 -> 14, of which waited for: 0 -> 6; matrix products, arithmetic and copies ran while one was open for 0% -> 0% of each run, Pallas kernels for 0% -> 10%
where the time goes in v2:
time: 27.2 us; the launch traced here: 27 us
  starting transfers between devices  13 us (48%)
  waiting for transfers between devices  7.51 us (28%)
  Pallas kernels  4.26 us (16%)
  between operations  2.13 us (8%)
    ppermute x4, starting transfers between devices, swap_chips(): return lax.ppermute(x, RANK_AXES, pairs)  7.35 us
    ppermute x3, starting transfers between devices, swap_tensor(): lax.ppermute(x, 'tensor', [(i, i ^ mask) for i in range(lax.axis_size('te...  4.57 us
    ppermute x4, waiting for transfers between devices, swap_chips(): return lax.ppermute(x, RANK_AXES, pairs)  4.18 us
    ppermute x3, waiting for transfers between devices, swap_tensor(): lax.ppermute(x, 'tensor', [(i, i ^ mask) for i in range(lax.axis_size('te...  2.07 us
    ppermute x7, waiting for transfers between devices, swap_cores(): return lax.ppermute(x, 'dp', [(i, i ^ 1) for i in range(count)])  1.26 us
    ppermute x7, starting transfers between devices, swap_cores(): return lax.ppermute(x, 'dp', [(i, i ^ 1) for i in range(count)])  1.04 us
    pallas_call x1, Pallas kernels, on_device(): call(functools.partial(order_kernel, chips, chunk), [((rows, columns), bf...  1.03 us
    pallas_call x1, Pallas kernels, on_device(): call(functools.partial(pair_kernel, chunk), [total], [VMEM] * 6, 'pair_to...  0.88 us
  transfers between devices with their start and end apart: 14, of which 6 were waited for; matrix products, arithmetic and copies ran while one was open for 0% of the time, Pallas kernels for 10%

profile of v2, /device:TPU:0, one launch (start us, length us, event | category | flops | bytes accessed | tf_op | source)
XLA Modules:
  0.0 27.0 jit_solution(6710549172480608928)
XLA Ops:
  0.7 3.0 %collective-permute-start.1 = (bf16[8,160]{1,0:T(8,128)(2,1)}, bf16[8,160]{1,0:T(8,128)(2,1)S(1)}, u32[]{:S(2)}, u32[]{:S(2)}) collective-permute-start(bf16[8,160]{1,0:T(8,128)(2,1)} %bitcast.29), channel_id=1, source_target_pairs={{0,16},{8,24},{16,0},{24,8},{1,17},{9,25},{17,1},{25,9},{2,18},{10... | collective-permute-start | bytes 7688 | tf_op jit(solution)/shard_map/ppermute | solution.py:53
  3.7 1.4 %collective-permute-start.2 = (bf16[8,160]{1,0:T(8,128)(2,1)}, bf16[8,160]{1,0:T(8,128)(2,1)S(1)}, u32[]{:S(2)}, u32[]{:S(2)}) collective-permute-start(bf16[8,160]{1,0:T(8,128)(2,1)} %bitcast.30), channel_id=1, source_target_pairs={{0,24},{8,16},{16,8},{24,0},{1,25},{9,17},{17,9},{25,1},{2,26},{10... | collective-permute-start | bytes 7688 | tf_op jit(solution)/shard_map/ppermute | solution.py:53
  5.1 0.1 collective-permute-start
  5.2 0.0 collective-permute-start.3
  5.2 0.5 %collective-permute-start.4 = (f32[1,7168]{1,0:T(1,128)}, f32[1,7168]{1,0:T(1,128)S(1)}, u32[]{:S(2)}, u32[]{:S(2)}) collective-permute-start(f32[1,7168]{1,0:T(1,128)} %bitcast.18), channel_id=1, source_target_pairs={{0,4},{4,0},{1,5},{5,1},{2,6},{6,2},{3,7},{7,3},{8,12},{12,8},{9,1... | collective-permute-start | bytes 86024 | tf_op jit(solution)/shard_map/ppermute | solution.py:39
  5.7 0.0 collective-permute-start.5
  5.8 0.0 copy-start.1
  5.8 0.0 copy-start.2
  5.8 0.0 copy-start.3
  5.8 0.5 %own_tokens.1.before_ref = f32[8,7168]{1,0:T(8,128)S(1)} custom-call(s32[8,8]{1,0:T(8,128)S(1)} %owners.1.table_ref, s32[1,8]{1,0:T(1,128)S(1)} %bitcast.24, bf16[8,160]{1,0:T(8,128)(2,1)S(1)} %bitcast.32, bf16[640,7168]{1,0:T(8,128)(2,1)S(1)} %bitcast.12), custom_call_target="tpu_custom_call" | custom-call | tf_op jit(solution)/shard_map/own_tokens/pallas_call | solution.py:278
  6.3 2.1 %collective-permute-done.2.odd_ref = bf16[8,160]{1,0:T(8,128)(2,1)S(1)} collective-permute-done((bf16[8,160]{1,0:T(8,128)(2,1)}, bf16[8,160]{1,0:T(8,128)(2,1)S(1)}, u32[]{:S(2)}, u32[]{:S(2)}) %collective-permute-start.2) | collective-permute-done | bytes 2592 | tf_op jit(solution)/shard_map/ppermute | solution.py:53
  8.4 0.9 %pair_tokens.1.before_ref = f32[8,7168]{1,0:T(8,128)S(1)} custom-call(s32[8,8]{1,0:T(8,128)S(1)} %owners.1.table_ref, s32[1,8]{1,0:T(1,128)S(1)} %bitcast.25, bf16[8,160]{1,0:T(8,128)(2,1)S(1)} %collective-permute-done.1.even_ref, bf16[8,160]{1,0:T(8,128)(2,1)S(1)} %collective-permute-done.2.odd_ref, bf16[640,7168]{1,0:T(8,128)(2,1)S(1)} %bitcast.13, ...), custom_call_target="tpu_custom_call" | custom-call | tf_op jit(solution)/shard_map/pair_tokens/pallas_call | solution.py:282
  9.3 0.0 collective-permute-done.3.refs_3_
  9.4 0.5 %last_tokens.1 = (f32[8,3584]{1,0:T(8,128)S(1)}, bf16[8,3584]{1,0:T(8,128)(2,1)S(1)}, f32[2,7168]{1,0:T(2,128)S(1)}, f32[2,7168]{1,0:T(2,128)S(1)}, f32[2,7168]{1,0:T(2,128)S(1)}) custom-call(s32[8,8]{1,0:T(8,128)S(1)} %owners.1.table_ref, s32[1,8]{1,0:T(1,128)S(1)} %bitcast.26, bf16[8,160]{1,0:T(8,128)(2,1)S(1)} %collective-permute-done.feature_ref, ...), custom_call_target="tpu_custom_call" | custom-call | tf_op jit(solution)/shard_map/last_tokens/pallas_call | solution.py:285
  9.9 0.1 collective-permute-start.6
  10.0 1.2 %collective-permute-done.6 = bf16[8,3584]{1,0:T(8,128)(2,1)S(1)} collective-permute-done((bf16[8,3584]{1,0:T(8,128)(2,1)S(1)}, bf16[8,3584]{1,0:T(8,128)(2,1)S(1)}, u32[]{:S(2)}, u32[]{:S(2)}) %collective-permute-start.6) | collective-permute-done | bytes 57376 | tf_op jit(solution)/shard_map/ppermute | solution.py:39
  11.2 2.7 %collective-permute-start.7 = (bf16[4,3584]{1,0:T(4,128)(2,1)S(1)}, bf16[4,3584]{1,0:T(4,128)(2,1)S(1)}, u32[]{:S(2)}, u32[]{:S(2)}) collective-permute-start(bf16[4,3584]{1,0:T(4,128)(2,1)S(1)} %slice.22), channel_id=1, source_target_pairs={{0,2},{1,3},{2,0},{3,1},{4,7},{5,6},{6,5},{7,4},{8,10},{9,11},{10,... | collective-permute-start | bytes 86024 | tf_op jit(solution)/shard_map/ppermute | solution.py:49
  13.9 1.6 %collective-permute-start.8 = (bf16[2,3584]{1,0:T(2,128)(2,1)S(1)}, bf16[2,3584]{1,0:T(2,128)(2,1)S(1)}, u32[]{:S(2)}, u32[]{:S(2)}) collective-permute-start(bf16[2,3584]{1,0:T(2,128)(2,1)S(1)} %slice.25), channel_id=1, source_target_pairs={{0,1},{1,0},{2,3},{3,2},{4,5},{5,4},{6,7},{7,6},{8,9},{9,8},{10,11... | collective-permute-start | bytes 43016 | tf_op jit(solution)/shard_map/ppermute | solution.py:49
  15.5 0.8 %collective-permute-done.7 = bf16[4,3584]{1,0:T(4,128)(2,1)S(1)} collective-permute-done((bf16[4,3584]{1,0:T(4,128)(2,1)S(1)}, bf16[4,3584]{1,0:T(4,128)(2,1)S(1)}, u32[]{:S(2)}, u32[]{:S(2)}) %collective-permute-start.7) | collective-permute-done | bytes 28704 | tf_op jit(solution)/shard_map/ppermute | solution.py:49
  16.4 1.4 %collective-permute-done.8 = bf16[2,3584]{1,0:T(2,128)(2,1)S(1)} collective-permute-done((bf16[2,3584]{1,0:T(2,128)(2,1)S(1)}, bf16[2,3584]{1,0:T(2,128)(2,1)S(1)}, u32[]{:S(2)}, u32[]{:S(2)}) %collective-permute-start.8) | collective-permute-done | bytes 14368 | tf_op jit(solution)/shard_map/ppermute | solution.py:49
  17.8 0.1 collective-permute-start.9
  19.2 0.1 chip_params.1
  19.4 1.1 %collective-permute-start.11 = (bf16[4,3584]{1,0:T(4,128)(2,1)S(1)}, bf16[4,3584]{1,0:T(4,128)(2,1)S(1)}, u32[]{:S(2)}, u32[]{:S(2)}) collective-permute-start(bf16[4,3584]{1,0:T(4,128)(2,1)S(1)} %get-tuple-element.21.own_ref), channel_id=1, source_target_pairs={{0,2},{1,3},{2,0},{3,1},{4,7},{5,6},{6,5},{7,4},{8,10},{9,11},{10,... | collective-permute-start | bytes 86024 | tf_op jit(solution)/shard_map/ppermute | solution.py:49
  20.5 1.9 %collective-permute-start.10 = (bf16[2,3584]{1,0:T(2,128)(2,1)S(1)}, bf16[2,3584]{1,0:T(2,128)(2,1)S(1)}, u32[]{:S(2)}, u32[]{:S(2)}) collective-permute-start(bf16[2,3584]{1,0:T(2,128)(2,1)S(1)} %get-tuple-element.22), channel_id=1, source_target_pairs={{0,1},{1,0},{2,3},{3,2},{4,5},{5,4},{6,7},{7,6},{8,9},{9,8},{10,11... | collective-permute-start | bytes 43016 | tf_op jit(solution)/shard_map/ppermute | solution.py:49
  22.4 1.8 %collective-permute-done.11.refs_0_ = bf16[4,3584]{1,0:T(4,128)(2,1)S(1)} collective-permute-done((bf16[4,3584]{1,0:T(4,128)(2,1)S(1)}, bf16[4,3584]{1,0:T(4,128)(2,1)S(1)}, u32[]{:S(2)}, u32[]{:S(2)}) %collective-permute-start.11) | collective-permute-done | bytes 28704 | tf_op jit(solution)/shard_map/ppermute | solution.py:49
  24.2 0.2 collective-permute-start.13
  24.5 0.2 collective-permute-done.10.half_ref
  24.7 0.1 collective-permute-start.12
  24.8 0.7 %own_state.1 = (f32[1,7168]{1,0:T(1,128)}, f32[1,7168]{1,0:T(1,128)}, f32[1,7168]{1,0:T(1,128)}, f32[1,7168]{1,0:T(1,128)}) custom-call(s32[1]{0:T(128)S(6)} %copy.13.step_ref, f32[1]{0:T(128)S(6)} %copy.14.rate_ref, f32[4,3584]{1,0:T(4,128)S(1)} %pad_maximum_fusion.sums_ref, f32[4,3584]{1,0:T(4,128)S(1)} %collective-permute-done.9.others_ref, ...), custom_call_target="tpu_custom_call" | custom-call | tf_op jit(solution)/shard_map/own_state/pallas_call | solution.py:307
  25.5 0.5 %early_rows.1.total_ref = f32[8,7168]{1,0:T(8,128)S(1)} custom-call(s32[1,8]{1,0:T(1,128)S(1)} %bitcast.27, bf16[4,3584]{1,0:T(4,128)(2,1)S(1)} %get-tuple-element.21.own_ref, bf16[2,3584]{1,0:T(2,128)(2,1)S(1)} %collective-permute-done.10.half_ref, bf16[4,3584]{1,0:T(4,128)(2,1)S(1)} %collective-permute-done.11.refs_0_), custom_call_target="tpu_custom_call" | custom-call | tf_op jit(solution)/shard_map/early_rows/pallas_call | solution.py:317
  26.0 0.0 collective-permute-done.13.refs_0_
  26.0 1.0 %row_order.1 = bf16[8,7168]{1,0:T(8,128)(2,1)} custom-call(s32[1,8]{1,0:T(1,128)S(1)} %bitcast.28, f32[8,7168]{1,0:T(8,128)S(1)} %early_rows.1.total_ref, bf16[2,3584]{1,0:T(2,128)(2,1)S(1)} %collective-permute-done.12.half_ref, bf16[4,3584]{1,0:T(4,128)(2,1)S(1)} %collective-permute-done.13.refs_0_), custom_call_target="tpu_custom_call" | custom-call | tf_op jit(solution)/shard_map/row_order/pallas_call | solution.py:320
  (23 shorter events, 0.2 us)
Async XLA Ops:
  0.6 5.1 %copy-start.5 = (bf16[1,160,8]{1,2,0:T(8,128)(2,1)S(1)}, bf16[1,160,8]{1,2,0:T(8,128)(2,1)}, u32[]{:S(2)}) copy-start(bf16[1,160,8]{1,2,0:T(8,128)(2,1)} %param.8) | copy-start | bytes 7684
  0.6 5.1 %copy-start.4 = (s32[8]{0:T(128)S(1)}, s32[8]{0:T(128)}, u32[]{:S(2)}) copy-start(s32[8]{0:T(128)} %param.13) | copy-start | bytes 100
  0.7 5.1 %copy-start = (bf16[1,640,7168]{2,1,0:T(8,128)(2,1)S(1)}, bf16[1,640,7168]{2,1,0:T(8,128)(2,1)}, u32[]{:S(2)}) copy-start(bf16[1,640,7168]{2,1,0:T(8,128)(2,1)} %param.9) | copy-start | bytes 27525124
  0.7 5.1 %collective-permute-start.1 = (bf16[8,160]{1,0:T(8,128)(2,1)}, bf16[8,160]{1,0:T(8,128)(2,1)S(1)}, u32[]{:S(2)}, u32[]{:S(2)}) collective-permute-start(bf16[8,160]{1,0:T(8,128)(2,1)} %bitcast.29), channel_id=1, source_target_pairs={{0,16},{8,24},{16,0},{24,8},{1,17},{9,25},{17,1},{25,9},{2,18},{10... | collective-permute-start | bytes 7688 | tf_op jit(solution)/shard_map/ppermute | solution.py:53
  3.7 4.7 %collective-permute-start.2 = (bf16[8,160]{1,0:T(8,128)(2,1)}, bf16[8,160]{1,0:T(8,128)(2,1)S(1)}, u32[]{:S(2)}, u32[]{:S(2)}) collective-permute-start(bf16[8,160]{1,0:T(8,128)(2,1)} %bitcast.30), channel_id=1, source_target_pairs={{0,24},{8,16},{16,8},{24,0},{1,25},{9,17},{17,9},{25,1},{2,26},{10... | collective-permute-start | bytes 7688 | tf_op jit(solution)/shard_map/ppermute | solution.py:53
  5.1 4.2 %collective-permute-start = (bf16[8,160]{1,0:T(8,128)(2,1)}, bf16[8,160]{1,0:T(8,128)(2,1)S(1)}, u32[]{:S(2)}, u32[]{:S(2)}) collective-permute-start(bf16[8,160]{1,0:T(8,128)(2,1)} %bitcast.31), channel_id=1, source_target_pairs={{0,8},{8,0},{16,24},{24,16},{1,9},{9,1},{17,25},{25,17},{2,10},{10... | collective-permute-start | bytes 7688 | tf_op jit(solution)/shard_map/ppermute | solution.py:53
  5.2 4.1 %collective-permute-start.3 = (f32[1,7168]{1,0:T(1,128)}, f32[1,7168]{1,0:T(1,128)S(1)}, u32[]{:S(2)}, u32[]{:S(2)}) collective-permute-start(f32[1,7168]{1,0:T(1,128)} %bitcast.15), channel_id=1, source_target_pairs={{0,4},{4,0},{1,5},{5,1},{2,6},{6,2},{3,7},{7,3},{8,12},{12,8},{9,1... | collective-permute-start | bytes 86024 | tf_op jit(solution)/shard_map/ppermute | solution.py:39
  5.2 4.1 %collective-permute-start.4 = (f32[1,7168]{1,0:T(1,128)}, f32[1,7168]{1,0:T(1,128)S(1)}, u32[]{:S(2)}, u32[]{:S(2)}) collective-permute-start(f32[1,7168]{1,0:T(1,128)} %bitcast.18), channel_id=1, source_target_pairs={{0,4},{4,0},{1,5},{5,1},{2,6},{6,2},{3,7},{7,3},{8,12},{12,8},{9,1... | collective-permute-start | bytes 86024 | tf_op jit(solution)/shard_map/ppermute | solution.py:39
  5.7 3.6 %collective-permute-start.5 = (f32[1,7168]{1,0:T(1,128)}, f32[1,7168]{1,0:T(1,128)S(1)}, u32[]{:S(2)}, u32[]{:S(2)}) collective-permute-start(f32[1,7168]{1,0:T(1,128)} %bitcast.21), channel_id=1, source_target_pairs={{0,4},{4,0},{1,5},{5,1},{2,6},{6,2},{3,7},{7,3},{8,12},{12,8},{9,1... | collective-permute-start | bytes 86024 | tf_op jit(solution)/shard_map/ppermute | solution.py:39
  5.8 3.5 %copy-start.1 = (f32[1,1,7168]{2,1,0:T(1,128)S(1)}, f32[1,1,7168]{2,1,0:T(1,128)}, u32[]{:S(2)}) copy-start(f32[1,1,7168]{2,1,0:T(1,128)} %param.10) | copy-start | bytes 86020
  5.8 3.5 %copy-start.2 = (f32[1,1,7168]{2,1,0:T(1,128)S(1)}, f32[1,1,7168]{2,1,0:T(1,128)}, u32[]{:S(2)}) copy-start(f32[1,1,7168]{2,1,0:T(1,128)} %param.11) | copy-start | bytes 86020
  5.8 3.5 %copy-start.3 = (f32[1,1,7168]{2,1,0:T(1,128)S(1)}, f32[1,1,7168]{2,1,0:T(1,128)}, u32[]{:S(2)}) copy-start(f32[1,1,7168]{2,1,0:T(1,128)} %param.12) | copy-start | bytes 86020
  9.9 1.3 %collective-permute-start.6 = (bf16[8,3584]{1,0:T(8,128)(2,1)S(1)}, bf16[8,3584]{1,0:T(8,128)(2,1)S(1)}, u32[]{:S(2)}, u32[]{:S(2)}) collective-permute-start(bf16[8,3584]{1,0:T(8,128)(2,1)S(1)} %get-tuple-element.17), channel_id=1, source_target_pairs={{0,4},{4,0},{1,5},{5,1},{2,6},{6,2},{3,7},{7,3},{8,12},{12,8},{9,1... | collective-permute-start | bytes 172040 | tf_op jit(solution)/shard_map/ppermute | solution.py:39
  11.2 5.1 %collective-permute-start.7 = (bf16[4,3584]{1,0:T(4,128)(2,1)S(1)}, bf16[4,3584]{1,0:T(4,128)(2,1)S(1)}, u32[]{:S(2)}, u32[]{:S(2)}) collective-permute-start(bf16[4,3584]{1,0:T(4,128)(2,1)S(1)} %slice.22), channel_id=1, source_target_pairs={{0,2},{1,3},{2,0},{3,1},{4,7},{5,6},{6,5},{7,4},{8,10},{9,11},{10,... | collective-permute-start | bytes 86024 | tf_op jit(solution)/shard_map/ppermute | solution.py:49
  13.9 3.9 %collective-permute-start.8 = (bf16[2,3584]{1,0:T(2,128)(2,1)S(1)}, bf16[2,3584]{1,0:T(2,128)(2,1)S(1)}, u32[]{:S(2)}, u32[]{:S(2)}) collective-permute-start(bf16[2,3584]{1,0:T(2,128)(2,1)S(1)} %slice.25), channel_id=1, source_target_pairs={{0,1},{1,0},{2,3},{3,2},{4,5},{5,4},{6,7},{7,6},{8,9},{9,8},{10,11... | collective-permute-start | bytes 43016 | tf_op jit(solution)/shard_map/ppermute | solution.py:49
  17.8 1.4 %collective-permute-start.9 = (f32[4,3584]{1,0:T(4,128)S(1)}, f32[4,3584]{1,0:T(4,128)S(1)}, u32[]{:S(2)}, u32[]{:S(2)}) collective-permute-start(f32[4,3584]{1,0:T(4,128)S(1)} %pad_maximum_fusion.sums_ref), channel_id=1, source_target_pairs={{0,4},{4,0},{1,5},{5,1},{2,6},{6,2},{3,7},{7,3},{8,12},{12,8},{9,1... | collective-permute-start | bytes 172040 | tf_op jit(solution)/shard_map/ppermute | solution.py:39
  19.4 4.9 %collective-permute-start.11 = (bf16[4,3584]{1,0:T(4,128)(2,1)S(1)}, bf16[4,3584]{1,0:T(4,128)(2,1)S(1)}, u32[]{:S(2)}, u32[]{:S(2)}) collective-permute-start(bf16[4,3584]{1,0:T(4,128)(2,1)S(1)} %get-tuple-element.21.own_ref), channel_id=1, source_target_pairs={{0,2},{1,3},{2,0},{3,1},{4,7},{5,6},{6,5},{7,4},{8,10},{9,11},{10,... | collective-permute-start | bytes 86024 | tf_op jit(solution)/shard_map/ppermute | solution.py:49
  20.5 4.2 %collective-permute-start.10 = (bf16[2,3584]{1,0:T(2,128)(2,1)S(1)}, bf16[2,3584]{1,0:T(2,128)(2,1)S(1)}, u32[]{:S(2)}, u32[]{:S(2)}) collective-permute-start(bf16[2,3584]{1,0:T(2,128)(2,1)S(1)} %get-tuple-element.22), channel_id=1, source_target_pairs={{0,1},{1,0},{2,3},{3,2},{4,5},{5,4},{6,7},{7,6},{8,9},{9,8},{10,11... | collective-permute-start | bytes 43016 | tf_op jit(solution)/shard_map/ppermute | solution.py:49
  24.2 1.8 %collective-permute-start.13 = (bf16[4,3584]{1,0:T(4,128)(2,1)S(1)}, bf16[4,3584]{1,0:T(4,128)(2,1)S(1)}, u32[]{:S(2)}, u32[]{:S(2)}) collective-permute-start(bf16[4,3584]{1,0:T(4,128)(2,1)S(1)} %collective-permute-done.11.refs_0_), channel_id=1, source_target_pairs={{0,4},{4,0},{1,5},{5,1},{2,6},{6,2},{3,7},{7,3},{8,12},{12,8},{9,1... | collective-permute-start | bytes 86024 | tf_op jit(solution)/shard_map/ppermute | solution.py:39
  24.7 1.3 %collective-permute-start.12 = (bf16[2,3584]{1,0:T(2,128)(2,1)S(1)}, bf16[2,3584]{1,0:T(2,128)(2,1)S(1)}, u32[]{:S(2)}, u32[]{:S(2)}) collective-permute-start(bf16[2,3584]{1,0:T(2,128)(2,1)S(1)} %collective-permute-done.10.half_ref), channel_id=1, source_target_pairs={{0,4},{4,0},{1,5},{5,1},{2,6},{6,2},{3,7},{7,3},{8,12},{12,8},{9,1... | collective-permute-start | bytes 43016 | tf_op jit(solution)/shard_map/ppermute | solution.py:39

commit v3 on v2

--- a/solution.py
+++ b/solution.py
@@ -81,11 +81,9 @@
     return jnp.dot(pick, features.astype(bf16), preferred_element_type=f32).astype(bf16)
 
 
-def token_rows(depth, mask, count=1):
-    first = jnp.bitwise_xor(lax.axis_index("tensor"), mask)
-    if count > 1:
-        first = first - lax.rem(first, count)
-    return pl.ds(pl.multiple_of(first * depth, 32), count * depth)
+def token_rows(depth, mask):
+    shard = jnp.bitwise_xor(lax.axis_index("tensor"), mask)
+    return pl.ds(pl.multiple_of(shard * depth, 32), depth)
 
 
 def own_kernel(chunk, table_ref, owner_ref, feature_ref, g_ref, *refs):
@@ -97,12 +95,9 @@
         total_ref[:, columns] = jnp.dot(features, g_ref[held, columns], preferred_element_type=f32)
 
 
-def pair_kernel(chunk, table_ref, owner_ref, even_ref, odd_ref, g_ref, before_ref, total_ref):
-    low = lax.rem(lax.axis_index("tensor"), 2)
-    even, odd = even_ref[...].astype(f32), odd_ref[...].astype(f32)
-    blocks = [jnp.where(low == 0, even, odd), jnp.where(low == 0, odd, even)]
-    features = ordered(table_ref, owner_ref, jnp.concatenate(blocks, axis=1))
-    held = token_rows(even_ref.shape[1], 2, 2)
+def add_kernel(chunk, mask, table_ref, owner_ref, feature_ref, g_ref, before_ref, total_ref):
+    features = ordered(table_ref, owner_ref, feature_ref[...])
+    held = token_rows(feature_ref.shape[1], mask)
     for k in range(total_ref.shape[1] // chunk):
         columns = pl.ds(k * chunk, chunk)
         part = jnp.dot(features, g_ref[held, columns], preferred_element_type=f32)
@@ -191,11 +186,12 @@
 
 
 def early_kernel(chips, chunk, owner_ref, own_ref, half_ref, *refs):
-    near_refs, total_ref = refs[:-1], refs[-1]
+    near_refs, (total_ref, pick_ref) = refs[:-2], refs[-2:]
     core, chip = where_am_i()
     half = half_ref.shape[1]
     served = chips - 2
     pick = picker(chips, total_ref.shape[0], owner_ref, core, chip)
+    pick_ref[...] = pick
     own = pick[:, 2 * served + 2 :]
     shared = pick[:, 2 * served : 2 * served + 2]
     for k in range(half // chunk):
@@ -213,36 +209,43 @@
         total_ref[:, other] = total_other
 
 
-def order_kernel(chips, chunk, owner_ref, total_ref, half_ref, *refs):
-    far_refs, out_ref = refs[:-1], refs[-1]
-    core, chip = where_am_i()
-    half = half_ref.shape[1]
+def order_kernel(chips, chunk, pick_ref, total_ref, far_ref, out_ref, rows_ref, sems):
+    core, _ = where_am_i()
+    half = far_ref.shape[1]
     served = chips - 2
-    pick = picker(chips, total_ref.shape[0], owner_ref, core, chip)
+    pick = pick_ref[...]
     shared = pick[:, 2 * served : 2 * served + 2]
-    for k in range(half // chunk):
-        mine, other, place = halves(core, half, chunk, k)
-        total = total_ref[:, mine]
-        total_other = total_ref[:, other] + jnp.dot(shared, half_ref[:, place], preferred_element_type=f32)
-        for p, far_ref in enumerate(far_refs):
-            far = pick[:, served + 2 * p : served + 2 * p + 2]
+    copies = []
+    for side in range(2):
+        for k in range(half // chunk):
+            *sides, place = halves(core, half, chunk, k)
             rows = far_ref[:, place].astype(f32)
-            total += jnp.dot(far, rows[:2].astype(bf16), preferred_element_type=f32)
-            total_other += jnp.dot(far, rows[2:].astype(bf16), preferred_element_type=f32)
-        out_ref[:, mine] = total.astype(bf16)
-        out_ref[:, other] = total_other.astype(bf16)
+            total = total_ref[:, sides[side]]
+            if side:
+                total += jnp.dot(shared, rows[:2].astype(bf16), preferred_element_type=f32)
+            for p in range(served // 2):
+                far = pick[:, served + 2 * p : served + 2 * p + 2]
+                first = 4 * p + (4 if side else 2)
+                total += jnp.dot(far, rows[first : first + 2].astype(bf16), preferred_element_type=f32)
+            rows_ref[:, sides[side]] = total.astype(bf16)
+        done = halves(core, half, half, 0)[side]
+        copies.append(pltpu.make_async_copy(rows_ref.at[:, done], out_ref.at[:, done], sems.at[side]))
+        copies[side].start()
+    for copy in copies:
+        copy.wait()
 
 
 VMEM = pl.BlockSpec(memory_space=pltpu.VMEM)
 SMEM = pl.BlockSpec(memory_space=pltpu.SMEM)
 
 
-def call(kernel, outs, specs, name, cost=None):
+def call(kernel, outs, specs, name, cost=None, out_spec=VMEM, scratch=()):
     return pl.pallas_call(
         kernel,
         out_shape=[jax.ShapeDtypeStruct(shape, dtype) for shape, dtype in outs],
         in_specs=specs,
-        out_specs=[VMEM] * len(outs),
+        out_specs=[out_spec] * len(outs),
+        scratch_shapes=scratch,
         compiler_params=pltpu.CompilerParams(vmem_limit_bytes=4 << 20),
         cost_estimate=cost,
         name=name,
@@ -272,16 +275,17 @@
         [((rows, rows), jnp.int32)],
         [],
         "owners",
-        pl.CostEstimate(flops=3_500_000_000, bytes_accessed=0, transcendentals=0),
+        pl.CostEstimate(flops=3_000_000_000, bytes_accessed=0, transcendentals=0),
     )()
     total = ((rows, columns), f32)
     (part,) = call(functools.partial(own_kernel, chunk), [total], [VMEM] * 4, "own_tokens")(
         table, owners, mine, source
     )
     partner = [swap_cores(x) for x in state]
-    (part,) = call(functools.partial(pair_kernel, chunk), [total], [VMEM] * 6, "pair_tokens")(
-        table, owners, next_two, diagonal, source, part
-    )
+    for mask, block, name in ((3, diagonal, "diagonal_tokens"), (2, next_two, "next_two_tokens")):
+        (part,) = call(functools.partial(add_kernel, chunk, mask), [total], [VMEM] * 5, name)(
+            table, owners, block, source, part
+        )
     keep, send, *state_rows = call(
         functools.partial(last_kernel, chips, chunk),
         [((2 * served + 4, half), f32), ((2 * served + 4, half), bf16)] + [((2, columns), f32)] * 3,
@@ -312,17 +316,22 @@
     )(step_count, learning_rate, *grads, *state)
     near = [swap_chips(params, *pair) for pair in pairs]
     near_half = swap_chips(params_half, SHARED, SHARED)
-    far = [swap_cores(x) for x in near]
-    far_half = swap_cores(near_half)
-    (early,) = call(
-        functools.partial(early_kernel, chips, chunk), [total], [VMEM] * (3 + len(near)), "early_rows"
+    far = swap_cores(jnp.concatenate([near_half, *near], axis=0))
+    early, pick = call(
+        functools.partial(early_kernel, chips, chunk),
+        [total, ((rows, rows), bf16)],
+        [VMEM] * (3 + len(near)),
+        "early_rows",
+        pl.CostEstimate(flops=5_000_000_000, bytes_accessed=0, transcendentals=0),
     )(owners, params, near_half, *near)
     (params,) = call(
         functools.partial(order_kernel, chips, chunk),
         [((rows, columns), bf16)],
-        [VMEM] * (3 + len(far)),
+        [VMEM] * 3,
         "row_order",
-    )(owners, early, far_half, *far)
+        out_spec=pl.BlockSpec(memory_space=pl.ANY),
+        scratch=[pltpu.VMEM((rows, columns), bf16), pltpu.SemaphoreType.DMA((2,))],
+    )(pick, early, far)
     return (params, *[x.reshape(master.shape) for x in outs])
 
 

time: 27.2 us -> 26.8 us (0.985)
  waiting for transfers between devices: 7.51 us -> 7.2 us
    ppermute x7 -> x6, waiting for transfers between devices: 1.26 us -> 1.91 us  [swap_cores(): return lax.ppermute(x, 'dp', [(i, i ^ 1) for i in range(count)])]
    ppermute x3, waiting for transfers between devices: 2.07 us -> 1.59 us  [swap_tensor(): lax.ppermute(x, 'tensor', [(i, i ^ mask) for i in range(lax.axis_size('te...]
    ppermute x4, waiting for transfers between devices: 4.18 us -> 3.71 us  [swap_chips(): return lax.ppermute(x, RANK_AXES, pairs)]
    ppermute x7 -> x6, starting transfers between devices: 1.04 us -> 0.86 us  [swap_cores(): return lax.ppermute(x, 'dp', [(i, i ^ 1) for i in range(count)])]
    pallas_call x2 -> x3, Pallas kernels: 1.35 us -> 1.48 us  [the longest x2 1.02 us: on_device(): call(functools.partial(add_kernel, chunk, mask), [total], [VMEM] * 5, name)]
  transfers between devices with their start and end apart: 14 -> 13, of which waited for: 6 -> 7; matrix products, arithmetic and copies ran while one was open for 0% -> 0% of each run, Pallas kernels for 10% -> 10%
where the time goes in v3:
time: 26.8 us; the launch traced here: 26.6 us
  starting transfers between devices  12.8 us (48%)
  waiting for transfers between devices  7.2 us (27%)
  Pallas kernels  4.3 us (16%)
  between operations  2.1 us (8%)
    ppermute x4, starting transfers between devices, swap_chips(): return lax.ppermute(x, RANK_AXES, pairs)  7.35 us
    ppermute x3, starting transfers between devices, swap_tensor(): lax.ppermute(x, 'tensor', [(i, i ^ mask) for i in range(lax.axis_size('te...  4.6 us
    ppermute x4, waiting for transfers between devices, swap_chips(): return lax.ppermute(x, RANK_AXES, pairs)  3.71 us
    ppermute x6, waiting for transfers between devices, swap_cores(): return lax.ppermute(x, 'dp', [(i, i ^ 1) for i in range(count)])  1.91 us
    ppermute x3, waiting for transfers between devices, swap_tensor(): lax.ppermute(x, 'tensor', [(i, i ^ mask) for i in range(lax.axis_size('te...  1.59 us
    pallas_call x2, Pallas kernels, on_device(): call(functools.partial(add_kernel, chunk, mask), [total], [VMEM] * 5, name)  1.02 us
    pallas_call x1, Pallas kernels, on_device(): call(functools.partial(order_kernel, chips, chunk), [((rows, columns), bf...  0.94 us
    ppermute x6, starting transfers between devices, swap_cores(): return lax.ppermute(x, 'dp', [(i, i ^ 1) for i in range(count)])  0.86 us
  transfers between devices with their start and end apart: 13, of which 7 were waited for; matrix products, arithmetic and copies ran while one was open for 0% of the time, Pallas kernels for 10%

profile of v3, /device:TPU:0, one launch (start us, length us, event | category | flops | bytes accessed | tf_op | source)
XLA Modules:
  0.0 26.6 jit_solution(7935046169494937387)
XLA Ops:
  0.7 4.0 %collective-permute-start.2 = (bf16[8,160]{1,0:T(8,128)(2,1)}, bf16[8,160]{1,0:T(8,128)(2,1)S(1)}, u32[]{:S(2)}, u32[]{:S(2)}) collective-permute-start(bf16[8,160]{1,0:T(8,128)(2,1)} %bitcast.30), channel_id=1, source_target_pairs={{0,24},{8,16},{16,8},{24,0},{1,25},{9,17},{17,9},{25,1},{2,26},{10... | collective-permute-start | bytes 7688 | tf_op jit(solution)/shard_map/ppermute | solution.py:53
  4.6 0.5 %collective-permute-start.1 = (bf16[8,160]{1,0:T(8,128)(2,1)}, bf16[8,160]{1,0:T(8,128)(2,1)S(1)}, u32[]{:S(2)}, u32[]{:S(2)}) collective-permute-start(bf16[8,160]{1,0:T(8,128)(2,1)} %bitcast.31), channel_id=1, source_target_pairs={{0,16},{8,24},{16,0},{24,8},{1,17},{9,25},{17,1},{25,9},{2,18},{10... | collective-permute-start | bytes 7688 | tf_op jit(solution)/shard_map/ppermute | solution.py:53
  5.1 0.1 collective-permute-start
  5.3 0.0 collective-permute-start.3
  5.3 0.5 %collective-permute-start.4 = (f32[1,7168]{1,0:T(1,128)}, f32[1,7168]{1,0:T(1,128)S(1)}, u32[]{:S(2)}, u32[]{:S(2)}) collective-permute-start(f32[1,7168]{1,0:T(1,128)} %bitcast.19), channel_id=1, source_target_pairs={{0,4},{4,0},{1,5},{5,1},{2,6},{6,2},{3,7},{7,3},{8,12},{12,8},{9,1... | collective-permute-start | bytes 86024 | tf_op jit(solution)/shard_map/ppermute | solution.py:39
  5.8 0.6 %collective-permute-done.2.feature_ref = bf16[8,160]{1,0:T(8,128)(2,1)S(1)} collective-permute-done((bf16[8,160]{1,0:T(8,128)(2,1)}, bf16[8,160]{1,0:T(8,128)(2,1)S(1)}, u32[]{:S(2)}, u32[]{:S(2)}) %collective-permute-start.2) | collective-permute-done | bytes 2592 | tf_op jit(solution)/shard_map/ppermute | solution.py:53
  6.4 0.0 collective-permute-start.5
  6.5 0.5 %own_tokens.1.before_ref = f32[8,7168]{1,0:T(8,128)S(1)} custom-call(s32[8,8]{1,0:T(8,128)S(1)} %owners.1.table_ref, s32[1,8]{1,0:T(1,128)S(1)} %bitcast.25, bf16[8,160]{1,0:T(8,128)(2,1)S(1)} %bitcast.33, bf16[640,7168]{1,0:T(8,128)(2,1)S(1)} %bitcast.12), custom_call_target="tpu_custom_call" | custom-call | tf_op jit(solution)/shard_map/own_tokens/pallas_call | solution.py:281
  7.0 0.5 %diagonal_tokens.1.before_ref = f32[8,7168]{1,0:T(8,128)S(1)} custom-call(s32[8,8]{1,0:T(8,128)S(1)} %owners.1.table_ref, s32[1,8]{1,0:T(1,128)S(1)} %bitcast.26, bf16[8,160]{1,0:T(8,128)(2,1)S(1)} %collective-permute-done.2.feature_ref, bf16[640,7168]{1,0:T(8,128)(2,1)S(1)} %bitcast.13, f32[8,7168]{1,0:T(8,128)S(1)} %own_tokens.1.before_ref), custom_call_target="tpu_custom_call" | custom-call | tf_op jit(solution)/shard_map/diagonal_tokens/pallas_call | solution.py:286
  7.5 0.9 %collective-permute-done.1.feature_ref = bf16[8,160]{1,0:T(8,128)(2,1)S(1)} collective-permute-done((bf16[8,160]{1,0:T(8,128)(2,1)}, bf16[8,160]{1,0:T(8,128)(2,1)S(1)}, u32[]{:S(2)}, u32[]{:S(2)}) %collective-permute-start.1) | collective-permute-done | bytes 2592 | tf_op jit(solution)/shard_map/ppermute | solution.py:53
  8.4 0.5 %next_two_tokens.1.before_ref = f32[8,7168]{1,0:T(8,128)S(1)} custom-call(s32[8,8]{1,0:T(8,128)S(1)} %owners.1.table_ref, s32[1,8]{1,0:T(1,128)S(1)} %bitcast.27, bf16[8,160]{1,0:T(8,128)(2,1)S(1)} %collective-permute-done.1.feature_ref, bf16[640,7168]{1,0:T(8,128)(2,1)S(1)} %bitcast.14, f32[8,7168]{1,0:T(8,128)S(1)} %diagonal_tokens.1.before_ref), custom_call_target="tpu_custom_call" | custom-call | tf_op jit(solution)/shard_map/next_two_tokens/pallas_call | solution.py:286
  8.9 0.0 collective-permute-done.feature_ref
  9.0 0.0 collective-permute-done.4.refs_4_
  9.0 0.5 %last_tokens.1 = (f32[8,3584]{1,0:T(8,128)S(1)}, bf16[8,3584]{1,0:T(8,128)(2,1)S(1)}, f32[2,7168]{1,0:T(2,128)S(1)}, f32[2,7168]{1,0:T(2,128)S(1)}, f32[2,7168]{1,0:T(2,128)S(1)}) custom-call(s32[8,8]{1,0:T(8,128)S(1)} %owners.1.table_ref, s32[1,8]{1,0:T(1,128)S(1)} %bitcast.28, bf16[8,160]{1,0:T(8,128)(2,1)S(1)} %collective-permute-done.feature_ref, ...), custom_call_target="tpu_custom_call" | custom-call | tf_op jit(solution)/shard_map/last_tokens/pallas_call | solution.py:289
  9.5 0.1 collective-permute-start.6
  9.6 1.2 %collective-permute-done.6 = bf16[8,3584]{1,0:T(8,128)(2,1)S(1)} collective-permute-done((bf16[8,3584]{1,0:T(8,128)(2,1)S(1)}, bf16[8,3584]{1,0:T(8,128)(2,1)S(1)}, u32[]{:S(2)}, u32[]{:S(2)}) %collective-permute-start.6) | collective-permute-done | bytes 57376 | tf_op jit(solution)/shard_map/ppermute | solution.py:39
  10.9 2.7 %collective-permute-start.7 = (bf16[4,3584]{1,0:T(4,128)(2,1)S(1)}, bf16[4,3584]{1,0:T(4,128)(2,1)S(1)}, u32[]{:S(2)}, u32[]{:S(2)}) collective-permute-start(bf16[4,3584]{1,0:T(4,128)(2,1)S(1)} %slice.22), channel_id=1, source_target_pairs={{0,2},{1,3},{2,0},{3,1},{4,7},{5,6},{6,5},{7,4},{8,10},{9,11},{10,... | collective-permute-start | bytes 86024 | tf_op jit(solution)/shard_map/ppermute | solution.py:49
  13.5 1.6 %collective-permute-start.8 = (bf16[2,3584]{1,0:T(2,128)(2,1)S(1)}, bf16[2,3584]{1,0:T(2,128)(2,1)S(1)}, u32[]{:S(2)}, u32[]{:S(2)}) collective-permute-start(bf16[2,3584]{1,0:T(2,128)(2,1)S(1)} %slice.25), channel_id=1, source_target_pairs={{0,1},{1,0},{2,3},{3,2},{4,5},{5,4},{6,7},{7,6},{8,9},{9,8},{10,11... | collective-permute-start | bytes 43016 | tf_op jit(solution)/shard_map/ppermute | solution.py:49
  15.2 0.8 %collective-permute-done.7 = bf16[4,3584]{1,0:T(4,128)(2,1)S(1)} collective-permute-done((bf16[4,3584]{1,0:T(4,128)(2,1)S(1)}, bf16[4,3584]{1,0:T(4,128)(2,1)S(1)}, u32[]{:S(2)}, u32[]{:S(2)}) %collective-permute-start.7) | collective-permute-done | bytes 28704 | tf_op jit(solution)/shard_map/ppermute | solution.py:49
  16.0 1.4 %collective-permute-done.8 = bf16[2,3584]{1,0:T(2,128)(2,1)S(1)} collective-permute-done((bf16[2,3584]{1,0:T(2,128)(2,1)S(1)}, bf16[2,3584]{1,0:T(2,128)(2,1)S(1)}, u32[]{:S(2)}, u32[]{:S(2)}) %collective-permute-start.8) | collective-permute-done | bytes 14368 | tf_op jit(solution)/shard_map/ppermute | solution.py:49
  17.5 0.1 collective-permute-start.9
  18.9 0.0 collective-permute-done.9.others_ref
  18.9 0.1 chip_params.1
  19.0 1.1 %collective-permute-start.11 = (bf16[4,3584]{1,0:T(4,128)(2,1)S(1)}, bf16[4,3584]{1,0:T(4,128)(2,1)S(1)}, u32[]{:S(2)}, u32[]{:S(2)}) collective-permute-start(bf16[4,3584]{1,0:T(4,128)(2,1)S(1)} %get-tuple-element.23.own_ref), channel_id=1, source_target_pairs={{0,2},{1,3},{2,0},{3,1},{4,7},{5,6},{6,5},{7,4},{8,10},{9,11},{10,... | collective-permute-start | bytes 86024 | tf_op jit(solution)/shard_map/ppermute | solution.py:49
  20.1 1.9 %collective-permute-start.10 = (bf16[2,3584]{1,0:T(2,128)(2,1)S(1)}, bf16[2,3584]{1,0:T(2,128)(2,1)S(1)}, u32[]{:S(2)}, u32[]{:S(2)}) collective-permute-start(bf16[2,3584]{1,0:T(2,128)(2,1)S(1)} %get-tuple-element.24), channel_id=1, source_target_pairs={{0,1},{1,0},{2,3},{3,2},{4,5},{5,4},{6,7},{7,6},{8,9},{9,8},{10,11... | collective-permute-start | bytes 43016 | tf_op jit(solution)/shard_map/ppermute | solution.py:49
  22.1 0.7 %own_state.1 = (f32[1,7168]{1,0:T(1,128)}, f32[1,7168]{1,0:T(1,128)}, f32[1,7168]{1,0:T(1,128)}, f32[1,7168]{1,0:T(1,128)}) custom-call(s32[1]{0:T(128)S(6)} %copy.13.step_ref, f32[1]{0:T(128)S(6)} %copy.14.rate_ref, f32[4,3584]{1,0:T(4,128)S(1)} %pad_maximum_fusion.sums_ref, f32[4,3584]{1,0:T(4,128)S(1)} %collective-permute-done.9.others_ref, ...), custom_call_target="tpu_custom_call" | custom-call | tf_op jit(solution)/shard_map/own_state/pallas_call | solution.py:311
  22.8 1.5 %collective-permute-done.10.half_ref = bf16[2,3584]{1,0:T(2,128)(2,1)S(1)} collective-permute-done((bf16[2,3584]{1,0:T(2,128)(2,1)S(1)}, bf16[2,3584]{1,0:T(2,128)(2,1)S(1)}, u32[]{:S(2)}, u32[]{:S(2)}) %collective-permute-start.10) | collective-permute-done | bytes 14368 | tf_op jit(solution)/shard_map/ppermute | solution.py:49
  24.3 0.0 collective-permute-done.11.refs_0_
  24.3 0.2 collective-permute-start.12
  24.5 0.5 %early_rows.1 = (f32[8,7168]{1,0:T(8,128)S(1)}, bf16[8,8]{1,0:T(8,128)(2,1)S(1)}) custom-call(s32[1,8]{1,0:T(1,128)S(1)} %bitcast.29, bf16[4,3584]{1,0:T(4,128)(2,1)S(1)} %get-tuple-element.23.own_ref, bf16[2,3584]{1,0:T(2,128)(2,1)S(1)} %collective-permute-done.10.half_ref, bf16[4,3584]{1,0:T(4,128)(2,1)S(1)} %collective-permute-done.11.refs_0_), custom_call_target="tpu_custom_call" | custom-call | flops 5000000000 | tf_op jit(solution)/shard_map/early_rows/pallas_call | solution.py:320
  25.0 0.7 %collective-permute-done.12.far_ref = bf16[6,3584]{1,0:T(8,128)(2,1)S(1)} collective-permute-done((bf16[6,3584]{1,0:T(8,128)(2,1)S(1)}, bf16[6,3584]{1,0:T(8,128)(2,1)S(1)}, u32[]{:S(2)}, u32[]{:S(2)}) %collective-permute-start.12) | collective-permute-done | bytes 43040 | tf_op jit(solution)/shard_map/ppermute | solution.py:39
  25.7 0.9 %row_order.1 = bf16[8,7168]{1,0:T(8,128)(2,1)} custom-call(bf16[8,8]{1,0:T(8,128)(2,1)S(1)} %get-tuple-element.25.pick_ref, f32[8,7168]{1,0:T(8,128)S(1)} %get-tuple-element.26.total_ref, bf16[6,3584]{1,0:T(8,128)(2,1)S(1)} %collective-permute-done.12.far_ref), custom_call_target="tpu_custom_call" | custom-call | tf_op jit(solution)/shard_map/row_order/pallas_call | solution.py:327
  (23 shorter events, 0.2 us)
Async XLA Ops:
  0.6 5.8 %copy-start.5 = (bf16[1,160,8]{1,2,0:T(8,128)(2,1)S(1)}, bf16[1,160,8]{1,2,0:T(8,128)(2,1)}, u32[]{:S(2)}) copy-start(bf16[1,160,8]{1,2,0:T(8,128)(2,1)} %param.8) | copy-start | bytes 7684
  0.6 5.8 %copy-start.4 = (s32[8]{0:T(128)S(1)}, s32[8]{0:T(128)}, u32[]{:S(2)}) copy-start(s32[8]{0:T(128)} %param.13) | copy-start | bytes 100
  0.7 5.8 %copy-start = (bf16[1,640,7168]{2,1,0:T(8,128)(2,1)S(1)}, bf16[1,640,7168]{2,1,0:T(8,128)(2,1)}, u32[]{:S(2)}) copy-start(bf16[1,640,7168]{2,1,0:T(8,128)(2,1)} %param.9) | copy-start | bytes 27525124
  0.7 5.8 %collective-permute-start.2 = (bf16[8,160]{1,0:T(8,128)(2,1)}, bf16[8,160]{1,0:T(8,128)(2,1)S(1)}, u32[]{:S(2)}, u32[]{:S(2)}) collective-permute-start(bf16[8,160]{1,0:T(8,128)(2,1)} %bitcast.30), channel_id=1, source_target_pairs={{0,24},{8,16},{16,8},{24,0},{1,25},{9,17},{17,9},{25,1},{2,26},{10... | collective-permute-start | bytes 7688 | tf_op jit(solution)/shard_map/ppermute | solution.py:53
  4.6 3.8 %collective-permute-start.1 = (bf16[8,160]{1,0:T(8,128)(2,1)}, bf16[8,160]{1,0:T(8,128)(2,1)S(1)}, u32[]{:S(2)}, u32[]{:S(2)}) collective-permute-start(bf16[8,160]{1,0:T(8,128)(2,1)} %bitcast.31), channel_id=1, source_target_pairs={{0,16},{8,24},{16,0},{24,8},{1,17},{9,25},{17,1},{25,9},{2,18},{10... | collective-permute-start | bytes 7688 | tf_op jit(solution)/shard_map/ppermute | solution.py:53
  5.1 3.8 %collective-permute-start = (bf16[8,160]{1,0:T(8,128)(2,1)}, bf16[8,160]{1,0:T(8,128)(2,1)S(1)}, u32[]{:S(2)}, u32[]{:S(2)}) collective-permute-start(bf16[8,160]{1,0:T(8,128)(2,1)} %bitcast.32), channel_id=1, source_target_pairs={{0,8},{8,0},{16,24},{24,16},{1,9},{9,1},{17,25},{25,17},{2,10},{10... | collective-permute-start | bytes 7688 | tf_op jit(solution)/shard_map/ppermute | solution.py:53
  5.3 3.7 %collective-permute-start.3 = (f32[1,7168]{1,0:T(1,128)}, f32[1,7168]{1,0:T(1,128)S(1)}, u32[]{:S(2)}, u32[]{:S(2)}) collective-permute-start(f32[1,7168]{1,0:T(1,128)} %bitcast.16), channel_id=1, source_target_pairs={{0,4},{4,0},{1,5},{5,1},{2,6},{6,2},{3,7},{7,3},{8,12},{12,8},{9,1... | collective-permute-start | bytes 86024 | tf_op jit(solution)/shard_map/ppermute | solution.py:39
  5.3 3.7 %collective-permute-start.4 = (f32[1,7168]{1,0:T(1,128)}, f32[1,7168]{1,0:T(1,128)S(1)}, u32[]{:S(2)}, u32[]{:S(2)}) collective-permute-start(f32[1,7168]{1,0:T(1,128)} %bitcast.19), channel_id=1, source_target_pairs={{0,4},{4,0},{1,5},{5,1},{2,6},{6,2},{3,7},{7,3},{8,12},{12,8},{9,1... | collective-permute-start | bytes 86024 | tf_op jit(solution)/shard_map/ppermute | solution.py:39
  6.4 2.6 %collective-permute-start.5 = (f32[1,7168]{1,0:T(1,128)}, f32[1,7168]{1,0:T(1,128)S(1)}, u32[]{:S(2)}, u32[]{:S(2)}) collective-permute-start(f32[1,7168]{1,0:T(1,128)} %bitcast.22), channel_id=1, source_target_pairs={{0,4},{4,0},{1,5},{5,1},{2,6},{6,2},{3,7},{7,3},{8,12},{12,8},{9,1... | collective-permute-start | bytes 86024 | tf_op jit(solution)/shard_map/ppermute | solution.py:39
  7.0 2.0 %copy-start.1 = (f32[1,1,7168]{2,1,0:T(1,128)S(1)}, f32[1,1,7168]{2,1,0:T(1,128)}, u32[]{:S(2)}) copy-start(f32[1,1,7168]{2,1,0:T(1,128)} %param.10) | copy-start | bytes 86020
  7.0 2.0 %copy-start.2 = (f32[1,1,7168]{2,1,0:T(1,128)S(1)}, f32[1,1,7168]{2,1,0:T(1,128)}, u32[]{:S(2)}) copy-start(f32[1,1,7168]{2,1,0:T(1,128)} %param.11) | copy-start | bytes 86020
  7.0 2.0 %copy-start.3 = (f32[1,1,7168]{2,1,0:T(1,128)S(1)}, f32[1,1,7168]{2,1,0:T(1,128)}, u32[]{:S(2)}) copy-start(f32[1,1,7168]{2,1,0:T(1,128)} %param.12) | copy-start | bytes 86020
  9.5 1.3 %collective-permute-start.6 = (bf16[8,3584]{1,0:T(8,128)(2,1)S(1)}, bf16[8,3584]{1,0:T(8,128)(2,1)S(1)}, u32[]{:S(2)}, u32[]{:S(2)}) collective-permute-start(bf16[8,3584]{1,0:T(8,128)(2,1)S(1)} %get-tuple-element.19), channel_id=1, source_target_pairs={{0,4},{4,0},{1,5},{5,1},{2,6},{6,2},{3,7},{7,3},{8,12},{12,8},{9,1... | collective-permute-start | bytes 172040 | tf_op jit(solution)/shard_map/ppermute | solution.py:39
  10.9 5.1 %collective-permute-start.7 = (bf16[4,3584]{1,0:T(4,128)(2,1)S(1)}, bf16[4,3584]{1,0:T(4,128)(2,1)S(1)}, u32[]{:S(2)}, u32[]{:S(2)}) collective-permute-start(bf16[4,3584]{1,0:T(4,128)(2,1)S(1)} %slice.22), channel_id=1, source_target_pairs={{0,2},{1,3},{2,0},{3,1},{4,7},{5,6},{6,5},{7,4},{8,10},{9,11},{10,... | collective-permute-start | bytes 86024 | tf_op jit(solution)/shard_map/ppermute | solution.py:49
  13.5 3.9 %collective-permute-start.8 = (bf16[2,3584]{1,0:T(2,128)(2,1)S(1)}, bf16[2,3584]{1,0:T(2,128)(2,1)S(1)}, u32[]{:S(2)}, u32[]{:S(2)}) collective-permute-start(bf16[2,3584]{1,0:T(2,128)(2,1)S(1)} %slice.25), channel_id=1, source_target_pairs={{0,1},{1,0},{2,3},{3,2},{4,5},{5,4},{6,7},{7,6},{8,9},{9,8},{10,11... | collective-permute-start | bytes 43016 | tf_op jit(solution)/shard_map/ppermute | solution.py:49
  17.5 1.4 %collective-permute-start.9 = (f32[4,3584]{1,0:T(4,128)S(1)}, f32[4,3584]{1,0:T(4,128)S(1)}, u32[]{:S(2)}, u32[]{:S(2)}) collective-permute-start(f32[4,3584]{1,0:T(4,128)S(1)} %pad_maximum_fusion.sums_ref), channel_id=1, source_target_pairs={{0,4},{4,0},{1,5},{5,1},{2,6},{6,2},{3,7},{7,3},{8,12},{12,8},{9,1... | collective-permute-start | bytes 172040 | tf_op jit(solution)/shard_map/ppermute | solution.py:39
  19.0 5.3 %collective-permute-start.11 = (bf16[4,3584]{1,0:T(4,128)(2,1)S(1)}, bf16[4,3584]{1,0:T(4,128)(2,1)S(1)}, u32[]{:S(2)}, u32[]{:S(2)}) collective-permute-start(bf16[4,3584]{1,0:T(4,128)(2,1)S(1)} %get-tuple-element.23.own_ref), channel_id=1, source_target_pairs={{0,2},{1,3},{2,0},{3,1},{4,7},{5,6},{6,5},{7,4},{8,10},{9,11},{10,... | collective-permute-start | bytes 86024 | tf_op jit(solution)/shard_map/ppermute | solution.py:49
  20.1 4.2 %collective-permute-start.10 = (bf16[2,3584]{1,0:T(2,128)(2,1)S(1)}, bf16[2,3584]{1,0:T(2,128)(2,1)S(1)}, u32[]{:S(2)}, u32[]{:S(2)}) collective-permute-start(bf16[2,3584]{1,0:T(2,128)(2,1)S(1)} %get-tuple-element.24), channel_id=1, source_target_pairs={{0,1},{1,0},{2,3},{3,2},{4,5},{5,4},{6,7},{7,6},{8,9},{9,8},{10,11... | collective-permute-start | bytes 43016 | tf_op jit(solution)/shard_map/ppermute | solution.py:49
  24.3 1.3 %collective-permute-start.12 = (bf16[6,3584]{1,0:T(8,128)(2,1)S(1)}, bf16[6,3584]{1,0:T(8,128)(2,1)S(1)}, u32[]{:S(2)}, u32[]{:S(2)}) collective-permute-start(bf16[6,3584]{1,0:T(8,128)(2,1)S(1)} %pad_maximum_fusion.1), channel_id=1, source_target_pairs={{0,4},{4,0},{1,5},{5,1},{2,6},{6,2},{3,7},{7,3},{8,12},{12,8},{9,1... | collective-permute-start | bytes 129032 | tf_op jit(solution)/shard_map/ppermute | solution.py:39

commit v4 on v3

--- a/solution.py
+++ b/solution.py
@@ -77,7 +77,11 @@
 
 
 def ordered(table_ref, owner_ref, features):
-    pick = (table_ref[...] == owner_ref[...]).astype(f32).astype(bf16)
+    pick = (table_ref[...] == owner_ref[...]).astype(f32)
+    if pick.shape[0] <= 16:
+        features = features.astype(f32)
+        return sum(pick[:, j : j + 1] * features[j : j + 1] for j in range(pick.shape[0])).astype(bf16)
+    pick = pick.astype(bf16)
     return jnp.dot(pick, features.astype(bf16), preferred_element_type=f32).astype(bf16)
 
 
@@ -186,14 +190,22 @@
 
 
 def early_kernel(chips, chunk, owner_ref, own_ref, half_ref, *refs):
-    near_refs, (total_ref, pick_ref) = refs[:-2], refs[-2:]
+    near_refs, (total_ref, mine_ref, other_ref) = refs[:-3], refs[-3:]
     core, chip = where_am_i()
     half = half_ref.shape[1]
+    rows = total_ref.shape[0]
     served = chips - 2
-    pick = picker(chips, total_ref.shape[0], owner_ref, core, chip)
-    pick_ref[...] = pick
+    pick = picker(chips, rows, owner_ref, core, chip)
     own = pick[:, 2 * served + 2 :]
     shared = pick[:, 2 * served : 2 * served + 2]
+    blank = jnp.zeros((rows, 2), f32)
+    mine_columns, other_columns = [blank], [shared.astype(f32)]
+    for p in range(served, 2 * served, 2):
+        far = pick[:, p : p + 2].astype(f32)
+        mine_columns += [far, blank]
+        other_columns += [blank, far]
+    mine_ref[...] = jnp.concatenate(mine_columns, axis=1).astype(bf16)
+    other_ref[...] = jnp.concatenate(other_columns, axis=1).astype(bf16)
     for k in range(half // chunk):
         mine, other, place = halves(core, half, chunk, k)
         rows = own_ref[:, place].astype(f32)
@@ -209,25 +221,16 @@
         total_ref[:, other] = total_other
 
 
-def order_kernel(chips, chunk, pick_ref, total_ref, far_ref, out_ref, rows_ref, sems):
+def order_kernel(chunk, mine_ref, other_ref, total_ref, far_ref, out_ref, rows_ref, sems):
     core, _ = where_am_i()
     half = far_ref.shape[1]
-    served = chips - 2
-    pick = pick_ref[...]
-    shared = pick[:, 2 * served : 2 * served + 2]
     copies = []
-    for side in range(2):
+    for side, pick_ref in enumerate((mine_ref, other_ref)):
+        pick = pick_ref[...]
         for k in range(half // chunk):
             *sides, place = halves(core, half, chunk, k)
-            rows = far_ref[:, place].astype(f32)
-            total = total_ref[:, sides[side]]
-            if side:
-                total += jnp.dot(shared, rows[:2].astype(bf16), preferred_element_type=f32)
-            for p in range(served // 2):
-                far = pick[:, served + 2 * p : served + 2 * p + 2]
-                first = 4 * p + (4 if side else 2)
-                total += jnp.dot(far, rows[first : first + 2].astype(bf16), preferred_element_type=f32)
-            rows_ref[:, sides[side]] = total.astype(bf16)
+            far = jnp.dot(pick, far_ref[:, place], preferred_element_type=f32)
+            rows_ref[:, sides[side]] = (total_ref[:, sides[side]] + far).astype(bf16)
         done = halves(core, half, half, 0)[side]
         copies.append(pltpu.make_async_copy(rows_ref.at[:, done], out_ref.at[:, done], sems.at[side]))
         copies[side].start()
@@ -317,21 +320,21 @@
     near = [swap_chips(params, *pair) for pair in pairs]
     near_half = swap_chips(params_half, SHARED, SHARED)
     far = swap_cores(jnp.concatenate([near_half, *near], axis=0))
-    early, pick = call(
+    early, *picks = call(
         functools.partial(early_kernel, chips, chunk),
-        [total, ((rows, rows), bf16)],
+        [total] + [((rows, 2 * served + 2), bf16)] * 2,
         [VMEM] * (3 + len(near)),
         "early_rows",
         pl.CostEstimate(flops=5_000_000_000, bytes_accessed=0, transcendentals=0),
     )(owners, params, near_half, *near)
     (params,) = call(
-        functools.partial(order_kernel, chips, chunk),
+        functools.partial(order_kernel, chunk),
         [((rows, columns), bf16)],
-        [VMEM] * 3,
+        [VMEM] * 4,
         "row_order",
         out_spec=pl.BlockSpec(memory_space=pl.ANY),
         scratch=[pltpu.VMEM((rows, columns), bf16), pltpu.SemaphoreType.DMA((2,))],
-    )(pick, early, far)
+    )(*picks, early, far)
     return (params, *[x.reshape(master.shape) for x in outs])
 
 

time: 26.8 us -> 26.6 us (level)
  no operation moved by 1% of the time
where the time goes in v4:
time: 26.6 us; the launch traced here: 26.4 us
  starting transfers between devices  12.8 us (48%)
  waiting for transfers between devices  7.3 us (27%)
  Pallas kernels  4.06 us (15%)
  between operations  2.08 us (8%)
    ppermute x4, starting transfers between devices, swap_chips(): return lax.ppermute(x, RANK_AXES, pairs)  7.35 us
    ppermute x3, starting transfers between devices, swap_tensor(): lax.ppermute(x, 'tensor', [(i, i ^ mask) for i in range(lax.axis_size('te...  4.6 us
    ppermute x4, waiting for transfers between devices, swap_chips(): return lax.ppermute(x, RANK_AXES, pairs)  3.71 us
    ppermute x6, waiting for transfers between devices, swap_cores(): return lax.ppermute(x, 'dp', [(i, i ^ 1) for i in range(count)])  1.9 us
    ppermute x3, waiting for transfers between devices, swap_tensor(): lax.ppermute(x, 'tensor', [(i, i ^ mask) for i in range(lax.axis_size('te...  1.69 us
    pallas_call x2, Pallas kernels, on_device(): call(functools.partial(add_kernel, chunk, mask), [total], [VMEM] * 5, name)  0.95 us
    ppermute x6, starting transfers between devices, swap_cores(): return lax.ppermute(x, 'dp', [(i, i ^ 1) for i in range(count)])  0.86 us
    pallas_call x1, Pallas kernels, on_device(): call(functools.partial(order_kernel, chunk), [((rows, columns), bf16)], [...  0.83 us
  transfers between devices with their start and end apart: 13, of which 7 were waited for; matrix products, arithmetic and copies ran while one was open for 0% of the time, Pallas kernels for 10%

profile of v4, /device:TPU:0, one launch (start us, length us, event | category | flops | bytes accessed | tf_op | source)
XLA Modules:
  0.0 26.4 jit_solution(6275765018070379345)
XLA Ops:
  0.7 4.0 %collective-permute-start.2 = (bf16[8,160]{1,0:T(8,128)(2,1)}, bf16[8,160]{1,0:T(8,128)(2,1)S(1)}, u32[]{:S(2)}, u32[]{:S(2)}) collective-permute-start(bf16[8,160]{1,0:T(8,128)(2,1)} %bitcast.30), channel_id=1, source_target_pairs={{0,24},{8,16},{16,8},{24,0},{1,25},{9,17},{17,9},{25,1},{2,26},{10... | collective-permute-start | bytes 7688 | tf_op jit(solution)/shard_map/ppermute | solution.py:53
  4.6 0.5 %collective-permute-start.1 = (bf16[8,160]{1,0:T(8,128)(2,1)}, bf16[8,160]{1,0:T(8,128)(2,1)S(1)}, u32[]{:S(2)}, u32[]{:S(2)}) collective-permute-start(bf16[8,160]{1,0:T(8,128)(2,1)} %bitcast.31), channel_id=1, source_target_pairs={{0,16},{8,24},{16,0},{24,8},{1,17},{9,25},{17,1},{25,9},{2,18},{10... | collective-permute-start | bytes 7688 | tf_op jit(solution)/shard_map/ppermute | solution.py:53
  5.1 0.1 collective-permute-start
  5.3 0.0 collective-permute-start.3
  5.3 0.5 %collective-permute-start.4 = (f32[1,7168]{1,0:T(1,128)}, f32[1,7168]{1,0:T(1,128)S(1)}, u32[]{:S(2)}, u32[]{:S(2)}) collective-permute-start(f32[1,7168]{1,0:T(1,128)} %bitcast.19), channel_id=1, source_target_pairs={{0,4},{4,0},{1,5},{5,1},{2,6},{6,2},{3,7},{7,3},{8,12},{12,8},{9,1... | collective-permute-start | bytes 86024 | tf_op jit(solution)/shard_map/ppermute | solution.py:39
  5.8 0.6 %collective-permute-done.2.feature_ref = bf16[8,160]{1,0:T(8,128)(2,1)S(1)} collective-permute-done((bf16[8,160]{1,0:T(8,128)(2,1)}, bf16[8,160]{1,0:T(8,128)(2,1)S(1)}, u32[]{:S(2)}, u32[]{:S(2)}) %collective-permute-start.2) | collective-permute-done | bytes 2592 | tf_op jit(solution)/shard_map/ppermute | solution.py:53
  6.4 0.0 collective-permute-start.5
  6.5 0.5 %own_tokens.1.before_ref = f32[8,7168]{1,0:T(8,128)S(1)} custom-call(s32[8,8]{1,0:T(8,128)S(1)} %owners.1.table_ref, s32[1,8]{1,0:T(1,128)S(1)} %bitcast.25, bf16[8,160]{1,0:T(8,128)(2,1)S(1)} %bitcast.33, bf16[640,7168]{1,0:T(8,128)(2,1)S(1)} %bitcast.12), custom_call_target="tpu_custom_call" | custom-call | tf_op jit(solution)/shard_map/own_tokens/pallas_call | solution.py:284
  6.9 0.5 %diagonal_tokens.1.before_ref = f32[8,7168]{1,0:T(8,128)S(1)} custom-call(s32[8,8]{1,0:T(8,128)S(1)} %owners.1.table_ref, s32[1,8]{1,0:T(1,128)S(1)} %bitcast.26, bf16[8,160]{1,0:T(8,128)(2,1)S(1)} %collective-permute-done.2.feature_ref, bf16[640,7168]{1,0:T(8,128)(2,1)S(1)} %bitcast.13, f32[8,7168]{1,0:T(8,128)S(1)} %own_tokens.1.before_ref), custom_call_target="tpu_custom_call" | custom-call | tf_op jit(solution)/shard_map/diagonal_tokens/pallas_call | solution.py:289
  7.4 1.0 %collective-permute-done.1.feature_ref = bf16[8,160]{1,0:T(8,128)(2,1)S(1)} collective-permute-done((bf16[8,160]{1,0:T(8,128)(2,1)}, bf16[8,160]{1,0:T(8,128)(2,1)S(1)}, u32[]{:S(2)}, u32[]{:S(2)}) %collective-permute-start.1) | collective-permute-done | bytes 2592 | tf_op jit(solution)/shard_map/ppermute | solution.py:53
  8.4 0.5 %next_two_tokens.1.before_ref = f32[8,7168]{1,0:T(8,128)S(1)} custom-call(s32[8,8]{1,0:T(8,128)S(1)} %owners.1.table_ref, s32[1,8]{1,0:T(1,128)S(1)} %bitcast.27, bf16[8,160]{1,0:T(8,128)(2,1)S(1)} %collective-permute-done.1.feature_ref, bf16[640,7168]{1,0:T(8,128)(2,1)S(1)} %bitcast.14, f32[8,7168]{1,0:T(8,128)S(1)} %diagonal_tokens.1.before_ref), custom_call_target="tpu_custom_call" | custom-call | tf_op jit(solution)/shard_map/next_two_tokens/pallas_call | solution.py:289
  8.9 0.0 collective-permute-done.feature_ref
  8.9 0.0 collective-permute-done.3.refs_3_
  9.0 0.5 %last_tokens.1 = (f32[8,3584]{1,0:T(8,128)S(1)}, bf16[8,3584]{1,0:T(8,128)(2,1)S(1)}, f32[2,7168]{1,0:T(2,128)S(1)}, f32[2,7168]{1,0:T(2,128)S(1)}, f32[2,7168]{1,0:T(2,128)S(1)}) custom-call(s32[8,8]{1,0:T(8,128)S(1)} %owners.1.table_ref, s32[1,8]{1,0:T(1,128)S(1)} %bitcast.28, bf16[8,160]{1,0:T(8,128)(2,1)S(1)} %collective-permute-done.feature_ref, ...), custom_call_target="tpu_custom_call" | custom-call | tf_op jit(solution)/shard_map/last_tokens/pallas_call | solution.py:292
  9.5 0.1 collective-permute-start.6
  9.5 1.2 %collective-permute-done.6 = bf16[8,3584]{1,0:T(8,128)(2,1)S(1)} collective-permute-done((bf16[8,3584]{1,0:T(8,128)(2,1)S(1)}, bf16[8,3584]{1,0:T(8,128)(2,1)S(1)}, u32[]{:S(2)}, u32[]{:S(2)}) %collective-permute-start.6) | collective-permute-done | bytes 57376 | tf_op jit(solution)/shard_map/ppermute | solution.py:39
  10.8 2.7 %collective-permute-start.7 = (bf16[4,3584]{1,0:T(4,128)(2,1)S(1)}, bf16[4,3584]{1,0:T(4,128)(2,1)S(1)}, u32[]{:S(2)}, u32[]{:S(2)}) collective-permute-start(bf16[4,3584]{1,0:T(4,128)(2,1)S(1)} %slice.22), channel_id=1, source_target_pairs={{0,2},{1,3},{2,0},{3,1},{4,7},{5,6},{6,5},{7,4},{8,10},{9,11},{10,... | collective-permute-start | bytes 86024 | tf_op jit(solution)/shard_map/ppermute | solution.py:49
  13.5 1.6 %collective-permute-start.8 = (bf16[2,3584]{1,0:T(2,128)(2,1)S(1)}, bf16[2,3584]{1,0:T(2,128)(2,1)S(1)}, u32[]{:S(2)}, u32[]{:S(2)}) collective-permute-start(bf16[2,3584]{1,0:T(2,128)(2,1)S(1)} %slice.25), channel_id=1, source_target_pairs={{0,1},{1,0},{2,3},{3,2},{4,5},{5,4},{6,7},{7,6},{8,9},{9,8},{10,11... | collective-permute-start | bytes 43016 | tf_op jit(solution)/shard_map/ppermute | solution.py:49
  15.1 0.8 %collective-permute-done.7 = bf16[4,3584]{1,0:T(4,128)(2,1)S(1)} collective-permute-done((bf16[4,3584]{1,0:T(4,128)(2,1)S(1)}, bf16[4,3584]{1,0:T(4,128)(2,1)S(1)}, u32[]{:S(2)}, u32[]{:S(2)}) %collective-permute-start.7) | collective-permute-done | bytes 28704 | tf_op jit(solution)/shard_map/ppermute | solution.py:49
  16.0 1.4 %collective-permute-done.8 = bf16[2,3584]{1,0:T(2,128)(2,1)S(1)} collective-permute-done((bf16[2,3584]{1,0:T(2,128)(2,1)S(1)}, bf16[2,3584]{1,0:T(2,128)(2,1)S(1)}, u32[]{:S(2)}, u32[]{:S(2)}) %collective-permute-start.8) | collective-permute-done | bytes 14368 | tf_op jit(solution)/shard_map/ppermute | solution.py:49
  17.4 0.1 collective-permute-start.9
  18.8 0.0 collective-permute-done.9.others_ref
  18.8 0.1 chip_params.1
  19.0 1.1 %collective-permute-start.11 = (bf16[4,3584]{1,0:T(4,128)(2,1)S(1)}, bf16[4,3584]{1,0:T(4,128)(2,1)S(1)}, u32[]{:S(2)}, u32[]{:S(2)}) collective-permute-start(bf16[4,3584]{1,0:T(4,128)(2,1)S(1)} %get-tuple-element.24.own_ref), channel_id=1, source_target_pairs={{0,2},{1,3},{2,0},{3,1},{4,7},{5,6},{6,5},{7,4},{8,10},{9,11},{10,... | collective-permute-start | bytes 86024 | tf_op jit(solution)/shard_map/ppermute | solution.py:49
  20.1 1.9 %collective-permute-start.10 = (bf16[2,3584]{1,0:T(2,128)(2,1)S(1)}, bf16[2,3584]{1,0:T(2,128)(2,1)S(1)}, u32[]{:S(2)}, u32[]{:S(2)}) collective-permute-start(bf16[2,3584]{1,0:T(2,128)(2,1)S(1)} %get-tuple-element.25), channel_id=1, source_target_pairs={{0,1},{1,0},{2,3},{3,2},{4,5},{5,4},{6,7},{7,6},{8,9},{9,8},{10,11... | collective-permute-start | bytes 43016 | tf_op jit(solution)/shard_map/ppermute | solution.py:49
  22.0 0.7 %own_state.1 = (f32[1,7168]{1,0:T(1,128)}, f32[1,7168]{1,0:T(1,128)}, f32[1,7168]{1,0:T(1,128)}, f32[1,7168]{1,0:T(1,128)}) custom-call(s32[1]{0:T(128)S(6)} %copy.13.step_ref, f32[1]{0:T(128)S(6)} %copy.14.rate_ref, f32[4,3584]{1,0:T(4,128)S(1)} %pad_maximum_fusion.sums_ref, f32[4,3584]{1,0:T(4,128)S(1)} %collective-permute-done.9.others_ref, ...), custom_call_target="tpu_custom_call" | custom-call | tf_op jit(solution)/shard_map/own_state/pallas_call | solution.py:314
  22.7 1.5 %collective-permute-done.10.half_ref = bf16[2,3584]{1,0:T(2,128)(2,1)S(1)} collective-permute-done((bf16[2,3584]{1,0:T(2,128)(2,1)S(1)}, bf16[2,3584]{1,0:T(2,128)(2,1)S(1)}, u32[]{:S(2)}, u32[]{:S(2)}) %collective-permute-start.10) | collective-permute-done | bytes 14368 | tf_op jit(solution)/shard_map/ppermute | solution.py:49
  24.3 0.0 collective-permute-done.11.refs_0_
  24.3 0.2 collective-permute-start.12
  24.5 0.5 %early_rows.1 = (f32[8,7168]{1,0:T(8,128)S(1)}, bf16[8,6]{1,0:T(8,128)(2,1)S(1)}, bf16[8,6]{1,0:T(8,128)(2,1)S(1)}) custom-call(s32[1,8]{1,0:T(1,128)S(1)} %bitcast.29, bf16[4,3584]{1,0:T(4,128)(2,1)S(1)} %get-tuple-element.24.own_ref, bf16[2,3584]{1,0:T(2,128)(2,1)S(1)} %collective-permute-done.10.half_ref, bf16[4,3584]{1,0:T(4,128)(2,1)S(1)} %collective-permute-done.11.refs_0_), custom_call_target="tpu_custom_call" | custom-call | flops 5000000000 | tf_op jit(solution)/shard_map/early_rows/pallas_call | solution.py:323
  24.9 0.7 %collective-permute-done.12.far_ref = bf16[6,3584]{1,0:T(8,128)(2,1)S(1)} collective-permute-done((bf16[6,3584]{1,0:T(8,128)(2,1)S(1)}, bf16[6,3584]{1,0:T(8,128)(2,1)S(1)}, u32[]{:S(2)}, u32[]{:S(2)}) %collective-permute-start.12) | collective-permute-done | bytes 43040 | tf_op jit(solution)/shard_map/ppermute | solution.py:39
  25.6 0.8 %row_order.1 = bf16[8,7168]{1,0:T(8,128)(2,1)} custom-call(bf16[8,6]{1,0:T(8,128)(2,1)S(1)} %get-tuple-element.26.mine_ref, bf16[8,6]{1,0:T(8,128)(2,1)S(1)} %get-tuple-element.27.other_ref, f32[8,7168]{1,0:T(8,128)S(1)} %get-tuple-element.28.total_ref, bf16[6,3584]{1,0:T(8,128)(2,1)S(1)} %collective-permute-done.12.far_ref), custom_call_target="tpu_custom_call" | custom-call | tf_op jit(solution)/shard_map/row_order/pallas_call | solution.py:330
  (23 shorter events, 0.2 us)
Async XLA Ops:
  0.6 5.8 %copy-start.5 = (bf16[1,160,8]{1,2,0:T(8,128)(2,1)S(1)}, bf16[1,160,8]{1,2,0:T(8,128)(2,1)}, u32[]{:S(2)}) copy-start(bf16[1,160,8]{1,2,0:T(8,128)(2,1)} %param.8) | copy-start | bytes 7684
  0.6 5.8 %copy-start.4 = (s32[8]{0:T(128)S(1)}, s32[8]{0:T(128)}, u32[]{:S(2)}) copy-start(s32[8]{0:T(128)} %param.13) | copy-start | bytes 100
  0.7 5.8 %copy-start = (bf16[1,640,7168]{2,1,0:T(8,128)(2,1)S(1)}, bf16[1,640,7168]{2,1,0:T(8,128)(2,1)}, u32[]{:S(2)}) copy-start(bf16[1,640,7168]{2,1,0:T(8,128)(2,1)} %param.9) | copy-start | bytes 27525124
  0.7 5.8 %collective-permute-start.2 = (bf16[8,160]{1,0:T(8,128)(2,1)}, bf16[8,160]{1,0:T(8,128)(2,1)S(1)}, u32[]{:S(2)}, u32[]{:S(2)}) collective-permute-start(bf16[8,160]{1,0:T(8,128)(2,1)} %bitcast.30), channel_id=1, source_target_pairs={{0,24},{8,16},{16,8},{24,0},{1,25},{9,17},{17,9},{25,1},{2,26},{10... | collective-permute-start | bytes 7688 | tf_op jit(solution)/shard_map/ppermute | solution.py:53
  4.6 3.8 %collective-permute-start.1 = (bf16[8,160]{1,0:T(8,128)(2,1)}, bf16[8,160]{1,0:T(8,128)(2,1)S(1)}, u32[]{:S(2)}, u32[]{:S(2)}) collective-permute-start(bf16[8,160]{1,0:T(8,128)(2,1)} %bitcast.31), channel_id=1, source_target_pairs={{0,16},{8,24},{16,0},{24,8},{1,17},{9,25},{17,1},{25,9},{2,18},{10... | collective-permute-start | bytes 7688 | tf_op jit(solution)/shard_map/ppermute | solution.py:53
  5.1 3.8 %collective-permute-start = (bf16[8,160]{1,0:T(8,128)(2,1)}, bf16[8,160]{1,0:T(8,128)(2,1)S(1)}, u32[]{:S(2)}, u32[]{:S(2)}) collective-permute-start(bf16[8,160]{1,0:T(8,128)(2,1)} %bitcast.32), channel_id=1, source_target_pairs={{0,8},{8,0},{16,24},{24,16},{1,9},{9,1},{17,25},{25,17},{2,10},{10... | collective-permute-start | bytes 7688 | tf_op jit(solution)/shard_map/ppermute | solution.py:53
  5.3 3.7 %collective-permute-start.3 = (f32[1,7168]{1,0:T(1,128)}, f32[1,7168]{1,0:T(1,128)S(1)}, u32[]{:S(2)}, u32[]{:S(2)}) collective-permute-start(f32[1,7168]{1,0:T(1,128)} %bitcast.16), channel_id=1, source_target_pairs={{0,4},{4,0},{1,5},{5,1},{2,6},{6,2},{3,7},{7,3},{8,12},{12,8},{9,1... | collective-permute-start | bytes 86024 | tf_op jit(solution)/shard_map/ppermute | solution.py:39
  5.3 3.7 %collective-permute-start.4 = (f32[1,7168]{1,0:T(1,128)}, f32[1,7168]{1,0:T(1,128)S(1)}, u32[]{:S(2)}, u32[]{:S(2)}) collective-permute-start(f32[1,7168]{1,0:T(1,128)} %bitcast.19), channel_id=1, source_target_pairs={{0,4},{4,0},{1,5},{5,1},{2,6},{6,2},{3,7},{7,3},{8,12},{12,8},{9,1... | collective-permute-start | bytes 86024 | tf_op jit(solution)/shard_map/ppermute | solution.py:39
  6.4 2.5 %collective-permute-start.5 = (f32[1,7168]{1,0:T(1,128)}, f32[1,7168]{1,0:T(1,128)S(1)}, u32[]{:S(2)}, u32[]{:S(2)}) collective-permute-start(f32[1,7168]{1,0:T(1,128)} %bitcast.22), channel_id=1, source_target_pairs={{0,4},{4,0},{1,5},{5,1},{2,6},{6,2},{3,7},{7,3},{8,12},{12,8},{9,1... | collective-permute-start | bytes 86024 | tf_op jit(solution)/shard_map/ppermute | solution.py:39
  6.9 2.0 %copy-start.1 = (f32[1,1,7168]{2,1,0:T(1,128)S(1)}, f32[1,1,7168]{2,1,0:T(1,128)}, u32[]{:S(2)}) copy-start(f32[1,1,7168]{2,1,0:T(1,128)} %param.10) | copy-start | bytes 86020
  6.9 2.0 %copy-start.2 = (f32[1,1,7168]{2,1,0:T(1,128)S(1)}, f32[1,1,7168]{2,1,0:T(1,128)}, u32[]{:S(2)}) copy-start(f32[1,1,7168]{2,1,0:T(1,128)} %param.11) | copy-start | bytes 86020
  6.9 2.0 %copy-start.3 = (f32[1,1,7168]{2,1,0:T(1,128)S(1)}, f32[1,1,7168]{2,1,0:T(1,128)}, u32[]{:S(2)}) copy-start(f32[1,1,7168]{2,1,0:T(1,128)} %param.12) | copy-start | bytes 86020
  9.5 1.3 %collective-permute-start.6 = (bf16[8,3584]{1,0:T(8,128)(2,1)S(1)}, bf16[8,3584]{1,0:T(8,128)(2,1)S(1)}, u32[]{:S(2)}, u32[]{:S(2)}) collective-permute-start(bf16[8,3584]{1,0:T(8,128)(2,1)S(1)} %get-tuple-element.20), channel_id=1, source_target_pairs={{0,4},{4,0},{1,5},{5,1},{2,6},{6,2},{3,7},{7,3},{8,12},{12,8},{9,1... | collective-permute-start | bytes 172040 | tf_op jit(solution)/shard_map/ppermute | solution.py:39
  10.8 5.1 %collective-permute-start.7 = (bf16[4,3584]{1,0:T(4,128)(2,1)S(1)}, bf16[4,3584]{1,0:T(4,128)(2,1)S(1)}, u32[]{:S(2)}, u32[]{:S(2)}) collective-permute-start(bf16[4,3584]{1,0:T(4,128)(2,1)S(1)} %slice.22), channel_id=1, source_target_pairs={{0,2},{1,3},{2,0},{3,1},{4,7},{5,6},{6,5},{7,4},{8,10},{9,11},{10,... | collective-permute-start | bytes 86024 | tf_op jit(solution)/shard_map/ppermute | solution.py:49
  13.5 3.9 %collective-permute-start.8 = (bf16[2,3584]{1,0:T(2,128)(2,1)S(1)}, bf16[2,3584]{1,0:T(2,128)(2,1)S(1)}, u32[]{:S(2)}, u32[]{:S(2)}) collective-permute-start(bf16[2,3584]{1,0:T(2,128)(2,1)S(1)} %slice.25), channel_id=1, source_target_pairs={{0,1},{1,0},{2,3},{3,2},{4,5},{5,4},{6,7},{7,6},{8,9},{9,8},{10,11... | collective-permute-start | bytes 43016 | tf_op jit(solution)/shard_map/ppermute | solution.py:49
  17.4 1.4 %collective-permute-start.9 = (f32[4,3584]{1,0:T(4,128)S(1)}, f32[4,3584]{1,0:T(4,128)S(1)}, u32[]{:S(2)}, u32[]{:S(2)}) collective-permute-start(f32[4,3584]{1,0:T(4,128)S(1)} %pad_maximum_fusion.sums_ref), channel_id=1, source_target_pairs={{0,4},{4,0},{1,5},{5,1},{2,6},{6,2},{3,7},{7,3},{8,12},{12,8},{9,1... | collective-permute-start | bytes 172040 | tf_op jit(solution)/shard_map/ppermute | solution.py:39
  19.0 5.3 %collective-permute-start.11 = (bf16[4,3584]{1,0:T(4,128)(2,1)S(1)}, bf16[4,3584]{1,0:T(4,128)(2,1)S(1)}, u32[]{:S(2)}, u32[]{:S(2)}) collective-permute-start(bf16[4,3584]{1,0:T(4,128)(2,1)S(1)} %get-tuple-element.24.own_ref), channel_id=1, source_target_pairs={{0,2},{1,3},{2,0},{3,1},{4,7},{5,6},{6,5},{7,4},{8,10},{9,11},{10,... | collective-permute-start | bytes 86024 | tf_op jit(solution)/shard_map/ppermute | solution.py:49
  20.1 4.2 %collective-permute-start.10 = (bf16[2,3584]{1,0:T(2,128)(2,1)S(1)}, bf16[2,3584]{1,0:T(2,128)(2,1)S(1)}, u32[]{:S(2)}, u32[]{:S(2)}) collective-permute-start(bf16[2,3584]{1,0:T(2,128)(2,1)S(1)} %get-tuple-element.25), channel_id=1, source_target_pairs={{0,1},{1,0},{2,3},{3,2},{4,5},{5,4},{6,7},{7,6},{8,9},{9,8},{10,11... | collective-permute-start | bytes 43016 | tf_op jit(solution)/shard_map/ppermute | solution.py:49
  24.3 1.3 %collective-permute-start.12 = (bf16[6,3584]{1,0:T(8,128)(2,1)S(1)}, bf16[6,3584]{1,0:T(8,128)(2,1)S(1)}, u32[]{:S(2)}, u32[]{:S(2)}) collective-permute-start(bf16[6,3584]{1,0:T(8,128)(2,1)S(1)} %pad_maximum_fusion.1), channel_id=1, source_target_pairs={{0,4},{4,0},{1,5},{5,1},{2,6},{6,2},{3,7},{7,3},{8,12},{12,8},{9,1... | collective-permute-start | bytes 129032 | tf_op jit(solution)/shard_map/ppermute | solution.py:39

commit v5 on v4

--- a/solution.py
+++ b/solution.py
@@ -13,12 +13,21 @@
 decay_rate = 0.1
 f32, bf16 = jnp.float32, jnp.bfloat16
 RANK_AXES = ("dp", "replica")
-SHARED = 1
-
-
-def chip_masks(chips):
-    rest = [m for m in range(1, chips) if m != SHARED]
-    return [(rest[i], rest[i + 1]) for i in range(0, len(rest), 2)]
+
+
+def chip_steps(chips):
+    if chips == 4:
+        return [(("shift", 1), ("mask", 2))], ("shift", 3)
+    rest = [("mask", m) for m in range(2, chips)]
+    return [(rest[i], rest[i + 1]) for i in range(0, len(rest), 2)], ("mask", 1)
+
+
+def hop(chip, step, chips, back=False):
+    kind, amount = step
+    if kind == "mask":
+        return chip ^ amount if isinstance(chip, int) else jnp.bitwise_xor(chip, amount)
+    amount = chips - amount if back else amount
+    return (chip + amount) % chips if isinstance(chip, int) else lax.rem(chip + amount, chips)
 
 
 def where_am_i():
@@ -39,12 +48,12 @@
     return lax.ppermute(x, "dp", [(i, i ^ 1) for i in range(count)])
 
 
-def swap_chips(x, mask_even, mask_odd):
-    replicas = lax.axis_size("replica")
+def swap_chips(x, even, odd):
+    replicas, count = lax.axis_size("replica"), lax.axis_size("dp")
     pairs = []
-    for dp in range(lax.axis_size("dp")):
+    for dp in range(count):
         for z in range(replicas):
-            chip = (dp // 2 * replicas + z) ^ (mask_odd if dp % 2 else mask_even)
+            chip = hop(dp // 2 * replicas + z, odd if dp % 2 else even, count // 2 * replicas)
             pairs.append((dp * replicas + z, (chip // replicas * 2 + dp % 2) * replicas + chip % replicas))
     return lax.ppermute(x, RANK_AXES, pairs)
 
@@ -53,16 +62,14 @@
     return lax.ppermute(x, "tensor", [(i, i ^ mask) for i in range(lax.axis_size("tensor"))])
 
 
-def owners_of(row, chips, core, chip):
-    half = chips - 2
-    pairs = chip_masks(chips)
-    mask = jnp.where(row < 2 * half + 2, SHARED, 0)
-    for p, (even, odd) in enumerate(pairs):
-        mine = jnp.where(core == 0, even, odd)
-        theirs = jnp.where(core == 0, odd, even)
-        mask = jnp.where(lax.div(row, 2) == p, mine, mask)
-        mask = jnp.where(lax.div(row, 2) == p + len(pairs), theirs, mask)
-    return rank_of(jnp.bitwise_xor(chip, mask), lax.rem(row, 2))
+def owners_of(row, chips, core, chip, back=False):
+    pairs, shared = chip_steps(chips)
+    target = jnp.where(row < 4 * len(pairs) + 2, hop(chip, shared, chips, back), chip)
+    for p, pair in enumerate(pairs):
+        even, odd = [hop(chip, step, chips, back) for step in pair]
+        target = jnp.where(lax.div(row, 2) == p, jnp.where(core == 0, even, odd), target)
+        target = jnp.where(lax.div(row, 2) == p + len(pairs), jnp.where(core == 0, odd, even), target)
+    return rank_of(target, lax.rem(row, 2))
 
 
 def halves(core, half, chunk, k):
@@ -185,7 +192,7 @@
 
 def picker(chips, rows, owner_ref, core, chip):
     column = lax.broadcasted_iota(jnp.int32, (rows, rows), 0)
-    hot = (owners_of(column, chips, core, chip) == owner_ref[...]).astype(f32).T
+    hot = (owners_of(column, chips, core, chip, True) == owner_ref[...]).astype(f32).T
     return hot.astype(bf16)
 
 
@@ -221,34 +228,27 @@
         total_ref[:, other] = total_other
 
 
-def order_kernel(chunk, mine_ref, other_ref, total_ref, far_ref, out_ref, rows_ref, sems):
+def order_kernel(chunk, mine_ref, other_ref, total_ref, far_ref, out_ref):
     core, _ = where_am_i()
     half = far_ref.shape[1]
-    copies = []
-    for side, pick_ref in enumerate((mine_ref, other_ref)):
-        pick = pick_ref[...]
-        for k in range(half // chunk):
-            *sides, place = halves(core, half, chunk, k)
+    picks = mine_ref[...], other_ref[...]
+    for k in range(half // chunk):
+        *sides, place = halves(core, half, chunk, k)
+        for pick, columns in zip(picks, sides):
             far = jnp.dot(pick, far_ref[:, place], preferred_element_type=f32)
-            rows_ref[:, sides[side]] = (total_ref[:, sides[side]] + far).astype(bf16)
-        done = halves(core, half, half, 0)[side]
-        copies.append(pltpu.make_async_copy(rows_ref.at[:, done], out_ref.at[:, done], sems.at[side]))
-        copies[side].start()
-    for copy in copies:
-        copy.wait()
+            out_ref[:, columns] = (total_ref[:, columns] + far).astype(bf16)
 
 
 VMEM = pl.BlockSpec(memory_space=pltpu.VMEM)
 SMEM = pl.BlockSpec(memory_space=pltpu.SMEM)
 
 
-def call(kernel, outs, specs, name, cost=None, out_spec=VMEM, scratch=()):
+def call(kernel, outs, specs, name, cost=None):
     return pl.pallas_call(
         kernel,
         out_shape=[jax.ShapeDtypeStruct(shape, dtype) for shape, dtype in outs],
         in_specs=specs,
-        out_specs=[out_spec] * len(outs),
-        scratch_shapes=scratch,
+        out_specs=[VMEM] * len(outs),
         compiler_params=pltpu.CompilerParams(vmem_limit_bytes=4 << 20),
         cost_estimate=cost,
         name=name,
@@ -266,7 +266,7 @@
     half = columns // 2
     served = chips - 2
     chunk = 512 if half % 512 == 0 else 128
-    pairs = chip_masks(chips)
+    pairs, shared = chip_steps(chips)
     source = output_grad[0]
     owners = owner_map.reshape(1, ranks)
 
@@ -298,7 +298,7 @@
 
     sums = keep + swap_cores(send).astype(f32)
     arrived = [swap_chips(sums[4 * p : 4 * p + 4].astype(bf16), *pair) for p, pair in enumerate(pairs)]
-    arrived_half = swap_chips(sums[2 * served : 2 * served + 2].astype(bf16), SHARED, SHARED)
+    arrived_half = swap_chips(sums[2 * served : 2 * served + 2].astype(bf16), shared, shared)
     sums_half = arrived_half.astype(f32) + sums[2 * served + 2 :]
     arrived = sum(x.astype(f32) for x in arrived)
     chip_sums = jnp.concatenate([arrived[:2], arrived[2:] + sums_half], axis=0)
@@ -318,7 +318,7 @@
         "own_state",
     )(step_count, learning_rate, *grads, *state)
     near = [swap_chips(params, *pair) for pair in pairs]
-    near_half = swap_chips(params_half, SHARED, SHARED)
+    near_half = swap_chips(params_half, shared, shared)
     far = swap_cores(jnp.concatenate([near_half, *near], axis=0))
     early, *picks = call(
         functools.partial(early_kernel, chips, chunk),
@@ -332,8 +332,6 @@
         [((rows, columns), bf16)],
         [VMEM] * 4,
         "row_order",
-        out_spec=pl.BlockSpec(memory_space=pl.ANY),
-        scratch=[pltpu.VMEM((rows, columns), bf16), pltpu.SemaphoreType.DMA((2,))],
     )(*picks, early, far)
     return (params, *[x.reshape(master.shape) for x in outs])
 

time: 26.6 us -> 26.4 us (level)
  waiting for transfers between devices: 7.3 us -> 6.72 us
  starting transfers between devices: 12.8 us -> 13.1 us
    ppermute x4, waiting for transfers between devices: 3.71 us -> 3.03 us  [swap_chips(): return lax.ppermute(x, RANK_AXES, pairs)]
    ppermute x4, starting transfers between devices: 7.35 us -> 7.82 us  [swap_chips(): return lax.ppermute(x, RANK_AXES, pairs)]
where the time goes in v5:
time: 26.4 us; the launch traced here: 26.2 us
  starting transfers between devices  13.1 us (50%)
  waiting for transfers between devices  6.72 us (25%)
  Pallas kernels  4.07 us (15%)
  between operations  2.1 us (8%)
    ppermute x4, starting transfers between devices, swap_chips(): return lax.ppermute(x, RANK_AXES, pairs)  7.82 us
    ppermute x3, starting transfers between devices, swap_tensor(): lax.ppermute(x, 'tensor', [(i, i ^ mask) for i in range(lax.axis_size('te...  4.6 us
    ppermute x4, waiting for transfers between devices, swap_chips(): return lax.ppermute(x, RANK_AXES, pairs)  3.03 us
    ppermute x6, waiting for transfers between devices, swap_cores(): return lax.ppermute(x, 'dp', [(i, i ^ 1) for i in range(count)])  1.99 us
    ppermute x3, waiting for transfers between devices, swap_tensor(): lax.ppermute(x, 'tensor', [(i, i ^ mask) for i in range(lax.axis_size('te...  1.69 us
    pallas_call x2, Pallas kernels, on_device(): call(functools.partial(add_kernel, chunk, mask), [total], [VMEM] * 5, name)  0.95 us
    pallas_call x1, Pallas kernels, on_device(): call(functools.partial(order_kernel, chunk), [((rows, columns), bf16)], [...  0.83 us
    pallas_call x1, Pallas kernels, on_device(): call(functools.partial(state_kernel, chunk, count), [((1, columns), f32)]...  0.72 us
  transfers between devices with their start and end apart: 13, of which 7 were waited for; matrix products, arithmetic and copies ran while one was open for 0% of the time, Pallas kernels for 10%

profile of v5, /device:TPU:0, one launch (start us, length us, event | category | flops | bytes accessed | tf_op | source)
XLA Modules:
  0.0 26.2 jit_solution(1705023211949918238)
XLA Ops:
  0.7 4.0 %collective-permute-start.2 = (bf16[8,160]{1,0:T(8,128)(2,1)}, bf16[8,160]{1,0:T(8,128)(2,1)S(1)}, u32[]{:S(2)}, u32[]{:S(2)}) collective-permute-start(bf16[8,160]{1,0:T(8,128)(2,1)} %bitcast.30), channel_id=1, source_target_pairs={{0,24},{8,16},{16,8},{24,0},{1,25},{9,17},{17,9},{25,1},{2,26},{10... | collective-permute-start | bytes 7688 | tf_op jit(solution)/shard_map/ppermute | solution.py:62
  4.6 0.5 %collective-permute-start.1 = (bf16[8,160]{1,0:T(8,128)(2,1)}, bf16[8,160]{1,0:T(8,128)(2,1)S(1)}, u32[]{:S(2)}, u32[]{:S(2)}) collective-permute-start(bf16[8,160]{1,0:T(8,128)(2,1)} %bitcast.31), channel_id=1, source_target_pairs={{0,16},{8,24},{16,0},{24,8},{1,17},{9,25},{17,1},{25,9},{2,18},{10... | collective-permute-start | bytes 7688 | tf_op jit(solution)/shard_map/ppermute | solution.py:62
  5.1 0.1 collective-permute-start
  5.3 0.0 collective-permute-start.3
  5.3 0.5 %collective-permute-start.4 = (f32[1,7168]{1,0:T(1,128)}, f32[1,7168]{1,0:T(1,128)S(1)}, u32[]{:S(2)}, u32[]{:S(2)}) collective-permute-start(f32[1,7168]{1,0:T(1,128)} %bitcast.19), channel_id=1, source_target_pairs={{0,4},{4,0},{1,5},{5,1},{2,6},{6,2},{3,7},{7,3},{8,12},{12,8},{9,1... | collective-permute-start | bytes 86024 | tf_op jit(solution)/shard_map/ppermute | solution.py:48
  5.8 0.6 %collective-permute-done.2.feature_ref = bf16[8,160]{1,0:T(8,128)(2,1)S(1)} collective-permute-done((bf16[8,160]{1,0:T(8,128)(2,1)}, bf16[8,160]{1,0:T(8,128)(2,1)S(1)}, u32[]{:S(2)}, u32[]{:S(2)}) %collective-permute-start.2) | collective-permute-done | bytes 2592 | tf_op jit(solution)/shard_map/ppermute | solution.py:62
  6.5 0.5 %own_tokens.1.before_ref = f32[8,7168]{1,0:T(8,128)S(1)} custom-call(s32[8,8]{1,0:T(8,128)S(1)} %owners.1.table_ref, s32[1,8]{1,0:T(1,128)S(1)} %bitcast.25, bf16[8,160]{1,0:T(8,128)(2,1)S(1)} %bitcast.33, bf16[640,7168]{1,0:T(8,128)(2,1)S(1)} %bitcast.12), custom_call_target="tpu_custom_call" | custom-call | tf_op jit(solution)/shard_map/own_tokens/pallas_call | solution.py:284
  6.9 0.5 %diagonal_tokens.1.before_ref = f32[8,7168]{1,0:T(8,128)S(1)} custom-call(s32[8,8]{1,0:T(8,128)S(1)} %owners.1.table_ref, s32[1,8]{1,0:T(1,128)S(1)} %bitcast.26, bf16[8,160]{1,0:T(8,128)(2,1)S(1)} %collective-permute-done.2.feature_ref, bf16[640,7168]{1,0:T(8,128)(2,1)S(1)} %bitcast.13, f32[8,7168]{1,0:T(8,128)S(1)} %own_tokens.1.before_ref), custom_call_target="tpu_custom_call" | custom-call | tf_op jit(solution)/shard_map/diagonal_tokens/pallas_call | solution.py:289
  7.4 1.0 %collective-permute-done.1.feature_ref = bf16[8,160]{1,0:T(8,128)(2,1)S(1)} collective-permute-done((bf16[8,160]{1,0:T(8,128)(2,1)}, bf16[8,160]{1,0:T(8,128)(2,1)S(1)}, u32[]{:S(2)}, u32[]{:S(2)}) %collective-permute-start.1) | collective-permute-done | bytes 2592 | tf_op jit(solution)/shard_map/ppermute | solution.py:62
  8.4 0.5 %next_two_tokens.1.before_ref = f32[8,7168]{1,0:T(8,128)S(1)} custom-call(s32[8,8]{1,0:T(8,128)S(1)} %owners.1.table_ref, s32[1,8]{1,0:T(1,128)S(1)} %bitcast.27, bf16[8,160]{1,0:T(8,128)(2,1)S(1)} %collective-permute-done.1.feature_ref, bf16[640,7168]{1,0:T(8,128)(2,1)S(1)} %bitcast.14, f32[8,7168]{1,0:T(8,128)S(1)} %diagonal_tokens.1.before_ref), custom_call_target="tpu_custom_call" | custom-call | tf_op jit(solution)/shard_map/next_two_tokens/pallas_call | solution.py:289
  8.9 0.0 collective-permute-done.feature_ref
  8.9 0.0 collective-permute-done.3.refs_3_
  8.9 0.0 collective-permute-done.4.refs_4_
  9.0 0.0 collective-permute-done.5.refs_5_
  9.0 0.5 %last_tokens.1 = (f32[8,3584]{1,0:T(8,128)S(1)}, bf16[8,3584]{1,0:T(8,128)(2,1)S(1)}, f32[2,7168]{1,0:T(2,128)S(1)}, f32[2,7168]{1,0:T(2,128)S(1)}, f32[2,7168]{1,0:T(2,128)S(1)}) custom-call(s32[8,8]{1,0:T(8,128)S(1)} %owners.1.table_ref, s32[1,8]{1,0:T(1,128)S(1)} %bitcast.28, bf16[8,160]{1,0:T(8,128)(2,1)S(1)} %collective-permute-done.feature_ref, ...), custom_call_target="tpu_custom_call" | custom-call | tf_op jit(solution)/shard_map/last_tokens/pallas_call | solution.py:292
  9.5 0.1 collective-permute-start.6
  9.5 1.2 %collective-permute-done.6 = bf16[8,3584]{1,0:T(8,128)(2,1)S(1)} collective-permute-done((bf16[8,3584]{1,0:T(8,128)(2,1)S(1)}, bf16[8,3584]{1,0:T(8,128)(2,1)S(1)}, u32[]{:S(2)}, u32[]{:S(2)}) %collective-permute-start.6) | collective-permute-done | bytes 57376 | tf_op jit(solution)/shard_map/ppermute | solution.py:48
  10.8 1.6 %collective-permute-start.7 = (bf16[4,3584]{1,0:T(4,128)(2,1)S(1)}, bf16[4,3584]{1,0:T(4,128)(2,1)S(1)}, u32[]{:S(2)}, u32[]{:S(2)}) collective-permute-start(bf16[4,3584]{1,0:T(4,128)(2,1)S(1)} %slice.22), channel_id=1, source_target_pairs={{0,1},{1,2},{2,3},{3,0},{4,6},{5,7},{6,4},{7,5},{8,9},{9,10},{10,1... | collective-permute-start | bytes 86024 | tf_op jit(solution)/shard_map/ppermute | solution.py:58
  12.5 2.3 %collective-permute-start.8 = (bf16[2,3584]{1,0:T(2,128)(2,1)S(1)}, bf16[2,3584]{1,0:T(2,128)(2,1)S(1)}, u32[]{:S(2)}, u32[]{:S(2)}) collective-permute-start(bf16[2,3584]{1,0:T(2,128)(2,1)S(1)} %slice.25), channel_id=1, source_target_pairs={{0,3},{1,0},{2,1},{3,2},{4,7},{5,4},{6,5},{7,6},{8,11},{9,8},{10,9... | collective-permute-start | bytes 43016 | tf_op jit(solution)/shard_map/ppermute | solution.py:58
  14.8 1.9 %collective-permute-done.7 = bf16[4,3584]{1,0:T(4,128)(2,1)S(1)} collective-permute-done((bf16[4,3584]{1,0:T(4,128)(2,1)S(1)}, bf16[4,3584]{1,0:T(4,128)(2,1)S(1)}, u32[]{:S(2)}, u32[]{:S(2)}) %collective-permute-start.7) | collective-permute-done | bytes 28704 | tf_op jit(solution)/shard_map/ppermute | solution.py:58
  16.6 0.0 collective-permute-done.8
  16.7 0.1 collective-permute-start.9
  18.1 0.1 chip_params.1
  18.2 1.3 %collective-permute-start.11 = (bf16[4,3584]{1,0:T(4,128)(2,1)S(1)}, bf16[4,3584]{1,0:T(4,128)(2,1)S(1)}, u32[]{:S(2)}, u32[]{:S(2)}) collective-permute-start(bf16[4,3584]{1,0:T(4,128)(2,1)S(1)} %get-tuple-element.24.own_ref), channel_id=1, source_target_pairs={{0,1},{1,2},{2,3},{3,0},{4,6},{5,7},{6,4},{7,5},{8,9},{9,10},{10,1... | collective-permute-start | bytes 86024 | tf_op jit(solution)/shard_map/ppermute | solution.py:58
  19.5 2.6 %collective-permute-start.10 = (bf16[2,3584]{1,0:T(2,128)(2,1)S(1)}, bf16[2,3584]{1,0:T(2,128)(2,1)S(1)}, u32[]{:S(2)}, u32[]{:S(2)}) collective-permute-start(bf16[2,3584]{1,0:T(2,128)(2,1)S(1)} %get-tuple-element.25), channel_id=1, source_target_pairs={{0,3},{1,0},{2,1},{3,2},{4,7},{5,4},{6,5},{7,6},{8,11},{9,8},{10,9... | collective-permute-start | bytes 43016 | tf_op jit(solution)/shard_map/ppermute | solution.py:58
  22.1 0.7 %own_state.1 = (f32[1,7168]{1,0:T(1,128)}, f32[1,7168]{1,0:T(1,128)}, f32[1,7168]{1,0:T(1,128)}, f32[1,7168]{1,0:T(1,128)}) custom-call(s32[1]{0:T(128)S(6)} %copy.13.step_ref, f32[1]{0:T(128)S(6)} %copy.14.rate_ref, f32[4,3584]{1,0:T(4,128)S(1)} %pad_maximum_fusion.sums_ref, f32[4,3584]{1,0:T(4,128)S(1)} %collective-permute-done.9.others_ref, ...), custom_call_target="tpu_custom_call" | custom-call | tf_op jit(solution)/shard_map/own_state/pallas_call | solution.py:314
  22.9 0.7 %collective-permute-done.10.half_ref = bf16[2,3584]{1,0:T(2,128)(2,1)S(1)} collective-permute-done((bf16[2,3584]{1,0:T(2,128)(2,1)S(1)}, bf16[2,3584]{1,0:T(2,128)(2,1)S(1)}, u32[]{:S(2)}, u32[]{:S(2)}) %collective-permute-start.10) | collective-permute-done | bytes 14368 | tf_op jit(solution)/shard_map/ppermute | solution.py:58
  23.6 0.5 %collective-permute-done.11.refs_0_ = bf16[4,3584]{1,0:T(4,128)(2,1)S(1)} collective-permute-done((bf16[4,3584]{1,0:T(4,128)(2,1)S(1)}, bf16[4,3584]{1,0:T(4,128)(2,1)S(1)}, u32[]{:S(2)}, u32[]{:S(2)}) %collective-permute-start.11) | collective-permute-done | bytes 28704 | tf_op jit(solution)/shard_map/ppermute | solution.py:58
  24.1 0.1 collective-permute-start.12
  24.2 0.5 %early_rows.1 = (f32[8,7168]{1,0:T(8,128)S(1)}, bf16[8,6]{1,0:T(8,128)(2,1)S(1)}, bf16[8,6]{1,0:T(8,128)(2,1)S(1)}) custom-call(s32[1,8]{1,0:T(1,128)S(1)} %bitcast.29, bf16[4,3584]{1,0:T(4,128)(2,1)S(1)} %get-tuple-element.24.own_ref, bf16[2,3584]{1,0:T(2,128)(2,1)S(1)} %collective-permute-done.10.half_ref, bf16[4,3584]{1,0:T(4,128)(2,1)S(1)} %collective-permute-done.11.refs_0_), custom_call_target="tpu_custom_call" | custom-call | flops 5000000000 | tf_op jit(solution)/shard_map/early_rows/pallas_call | solution.py:323
  24.6 0.8 %collective-permute-done.12.far_ref = bf16[6,3584]{1,0:T(8,128)(2,1)S(1)} collective-permute-done((bf16[6,3584]{1,0:T(8,128)(2,1)S(1)}, bf16[6,3584]{1,0:T(8,128)(2,1)S(1)}, u32[]{:S(2)}, u32[]{:S(2)}) %collective-permute-start.12) | collective-permute-done | bytes 43040 | tf_op jit(solution)/shard_map/ppermute | solution.py:48
  25.4 0.8 %row_order.1 = bf16[8,7168]{1,0:T(8,128)(2,1)} custom-call(bf16[8,6]{1,0:T(8,128)(2,1)S(1)} %get-tuple-element.26.mine_ref, bf16[8,6]{1,0:T(8,128)(2,1)S(1)} %get-tuple-element.27.other_ref, f32[8,7168]{1,0:T(8,128)S(1)} %get-tuple-element.28.total_ref, bf16[6,3584]{1,0:T(8,128)(2,1)S(1)} %collective-permute-done.12.far_ref), custom_call_target="tpu_custom_call" | custom-call | tf_op jit(solution)/shard_map/row_order/pallas_call | solution.py:330
  (23 shorter events, 0.2 us)
Async XLA Ops:
  0.6 5.8 %copy-start.5 = (bf16[1,160,8]{1,2,0:T(8,128)(2,1)S(1)}, bf16[1,160,8]{1,2,0:T(8,128)(2,1)}, u32[]{:S(2)}) copy-start(bf16[1,160,8]{1,2,0:T(8,128)(2,1)} %param.8) | copy-start | bytes 7684
  0.6 5.8 %copy-start.4 = (s32[8]{0:T(128)S(1)}, s32[8]{0:T(128)}, u32[]{:S(2)}) copy-start(s32[8]{0:T(128)} %param.13) | copy-start | bytes 100
  0.7 5.8 %copy-start = (bf16[1,640,7168]{2,1,0:T(8,128)(2,1)S(1)}, bf16[1,640,7168]{2,1,0:T(8,128)(2,1)}, u32[]{:S(2)}) copy-start(bf16[1,640,7168]{2,1,0:T(8,128)(2,1)} %param.9) | copy-start | bytes 27525124
  0.7 5.8 %collective-permute-start.2 = (bf16[8,160]{1,0:T(8,128)(2,1)}, bf16[8,160]{1,0:T(8,128)(2,1)S(1)}, u32[]{:S(2)}, u32[]{:S(2)}) collective-permute-start(bf16[8,160]{1,0:T(8,128)(2,1)} %bitcast.30), channel_id=1, source_target_pairs={{0,24},{8,16},{16,8},{24,0},{1,25},{9,17},{17,9},{25,1},{2,26},{10... | collective-permute-start | bytes 7688 | tf_op jit(solution)/shard_map/ppermute | solution.py:62
  4.6 3.8 %collective-permute-start.1 = (bf16[8,160]{1,0:T(8,128)(2,1)}, bf16[8,160]{1,0:T(8,128)(2,1)S(1)}, u32[]{:S(2)}, u32[]{:S(2)}) collective-permute-start(bf16[8,160]{1,0:T(8,128)(2,1)} %bitcast.31), channel_id=1, source_target_pairs={{0,16},{8,24},{16,0},{24,8},{1,17},{9,25},{17,1},{25,9},{2,18},{10... | collective-permute-start | bytes 7688 | tf_op jit(solution)/shard_map/ppermute | solution.py:62
  5.1 3.8 %collective-permute-start = (bf16[8,160]{1,0:T(8,128)(2,1)}, bf16[8,160]{1,0:T(8,128)(2,1)S(1)}, u32[]{:S(2)}, u32[]{:S(2)}) collective-permute-start(bf16[8,160]{1,0:T(8,128)(2,1)} %bitcast.32), channel_id=1, source_target_pairs={{0,8},{8,0},{16,24},{24,16},{1,9},{9,1},{17,25},{25,17},{2,10},{10... | collective-permute-start | bytes 7688 | tf_op jit(solution)/shard_map/ppermute | solution.py:62
  5.3 3.7 %collective-permute-start.3 = (f32[1,7168]{1,0:T(1,128)}, f32[1,7168]{1,0:T(1,128)S(1)}, u32[]{:S(2)}, u32[]{:S(2)}) collective-permute-start(f32[1,7168]{1,0:T(1,128)} %bitcast.16), channel_id=1, source_target_pairs={{0,4},{4,0},{1,5},{5,1},{2,6},{6,2},{3,7},{7,3},{8,12},{12,8},{9,1... | collective-permute-start | bytes 86024 | tf_op jit(solution)/shard_map/ppermute | solution.py:48
  5.3 3.7 %collective-permute-start.4 = (f32[1,7168]{1,0:T(1,128)}, f32[1,7168]{1,0:T(1,128)S(1)}, u32[]{:S(2)}, u32[]{:S(2)}) collective-permute-start(f32[1,7168]{1,0:T(1,128)} %bitcast.19), channel_id=1, source_target_pairs={{0,4},{4,0},{1,5},{5,1},{2,6},{6,2},{3,7},{7,3},{8,12},{12,8},{9,1... | collective-permute-start | bytes 86024 | tf_op jit(solution)/shard_map/ppermute | solution.py:48
  6.4 2.5 %collective-permute-start.5 = (f32[1,7168]{1,0:T(1,128)}, f32[1,7168]{1,0:T(1,128)S(1)}, u32[]{:S(2)}, u32[]{:S(2)}) collective-permute-start(f32[1,7168]{1,0:T(1,128)} %bitcast.22), channel_id=1, source_target_pairs={{0,4},{4,0},{1,5},{5,1},{2,6},{6,2},{3,7},{7,3},{8,12},{12,8},{9,1... | collective-permute-start | bytes 86024 | tf_op jit(solution)/shard_map/ppermute | solution.py:48
  6.9 2.0 %copy-start.1 = (f32[1,1,7168]{2,1,0:T(1,128)S(1)}, f32[1,1,7168]{2,1,0:T(1,128)}, u32[]{:S(2)}) copy-start(f32[1,1,7168]{2,1,0:T(1,128)} %param.10) | copy-start | bytes 86020
  6.9 2.0 %copy-start.2 = (f32[1,1,7168]{2,1,0:T(1,128)S(1)}, f32[1,1,7168]{2,1,0:T(1,128)}, u32[]{:S(2)}) copy-start(f32[1,1,7168]{2,1,0:T(1,128)} %param.11) | copy-start | bytes 86020
  6.9 2.0 %copy-start.3 = (f32[1,1,7168]{2,1,0:T(1,128)S(1)}, f32[1,1,7168]{2,1,0:T(1,128)}, u32[]{:S(2)}) copy-start(f32[1,1,7168]{2,1,0:T(1,128)} %param.12) | copy-start | bytes 86020
  9.5 1.3 %collective-permute-start.6 = (bf16[8,3584]{1,0:T(8,128)(2,1)S(1)}, bf16[8,3584]{1,0:T(8,128)(2,1)S(1)}, u32[]{:S(2)}, u32[]{:S(2)}) collective-permute-start(bf16[8,3584]{1,0:T(8,128)(2,1)S(1)} %get-tuple-element.20), channel_id=1, source_target_pairs={{0,4},{4,0},{1,5},{5,1},{2,6},{6,2},{3,7},{7,3},{8,12},{12,8},{9,1... | collective-permute-start | bytes 172040 | tf_op jit(solution)/shard_map/ppermute | solution.py:48
  10.8 5.8 %collective-permute-start.7 = (bf16[4,3584]{1,0:T(4,128)(2,1)S(1)}, bf16[4,3584]{1,0:T(4,128)(2,1)S(1)}, u32[]{:S(2)}, u32[]{:S(2)}) collective-permute-start(bf16[4,3584]{1,0:T(4,128)(2,1)S(1)} %slice.22), channel_id=1, source_target_pairs={{0,1},{1,2},{2,3},{3,0},{4,6},{5,7},{6,4},{7,5},{8,9},{9,10},{10,1... | collective-permute-start | bytes 86024 | tf_op jit(solution)/shard_map/ppermute | solution.py:58
  12.5 4.2 %collective-permute-start.8 = (bf16[2,3584]{1,0:T(2,128)(2,1)S(1)}, bf16[2,3584]{1,0:T(2,128)(2,1)S(1)}, u32[]{:S(2)}, u32[]{:S(2)}) collective-permute-start(bf16[2,3584]{1,0:T(2,128)(2,1)S(1)} %slice.25), channel_id=1, source_target_pairs={{0,3},{1,0},{2,1},{3,2},{4,7},{5,4},{6,5},{7,6},{8,11},{9,8},{10,9... | collective-permute-start | bytes 43016 | tf_op jit(solution)/shard_map/ppermute | solution.py:58
  16.7 1.4 %collective-permute-start.9 = (f32[4,3584]{1,0:T(4,128)S(1)}, f32[4,3584]{1,0:T(4,128)S(1)}, u32[]{:S(2)}, u32[]{:S(2)}) collective-permute-start(f32[4,3584]{1,0:T(4,128)S(1)} %pad_maximum_fusion.sums_ref), channel_id=1, source_target_pairs={{0,4},{4,0},{1,5},{5,1},{2,6},{6,2},{3,7},{7,3},{8,12},{12,8},{9,1... | collective-permute-start | bytes 172040 | tf_op jit(solution)/shard_map/ppermute | solution.py:48
  18.2 5.8 %collective-permute-start.11 = (bf16[4,3584]{1,0:T(4,128)(2,1)S(1)}, bf16[4,3584]{1,0:T(4,128)(2,1)S(1)}, u32[]{:S(2)}, u32[]{:S(2)}) collective-permute-start(bf16[4,3584]{1,0:T(4,128)(2,1)S(1)} %get-tuple-element.24.own_ref), channel_id=1, source_target_pairs={{0,1},{1,2},{2,3},{3,0},{4,6},{5,7},{6,4},{7,5},{8,9},{9,10},{10,1... | collective-permute-start | bytes 86024 | tf_op jit(solution)/shard_map/ppermute | solution.py:58
  19.5 4.0 %collective-permute-start.10 = (bf16[2,3584]{1,0:T(2,128)(2,1)S(1)}, bf16[2,3584]{1,0:T(2,128)(2,1)S(1)}, u32[]{:S(2)}, u32[]{:S(2)}) collective-permute-start(bf16[2,3584]{1,0:T(2,128)(2,1)S(1)} %get-tuple-element.25), channel_id=1, source_target_pairs={{0,3},{1,0},{2,1},{3,2},{4,7},{5,4},{6,5},{7,6},{8,11},{9,8},{10,9... | collective-permute-start | bytes 43016 | tf_op jit(solution)/shard_map/ppermute | solution.py:58
  24.1 1.3 %collective-permute-start.12 = (bf16[6,3584]{1,0:T(8,128)(2,1)S(1)}, bf16[6,3584]{1,0:T(8,128)(2,1)S(1)}, u32[]{:S(2)}, u32[]{:S(2)}) collective-permute-start(bf16[6,3584]{1,0:T(8,128)(2,1)S(1)} %pad_maximum_fusion.1), channel_id=1, source_target_pairs={{0,4},{4,0},{1,5},{5,1},{2,6},{6,2},{3,7},{7,3},{8,12},{12,8},{9,1... | collective-permute-start | bytes 129032 | tf_op jit(solution)/shard_map/ppermute | solution.py:48
